TPU v7x, 32 devices: a whole 2x2x4 slice. The times are simulated.
32 devices in a mesh: dp: 4 (over y, x), seq: 8 (over z, core).
Axes of the slice: x: 2, y: 2, z: 4, core: 2. Of those that a mesh axis runs over, the one named last changes fastest.
Arguments:
- latents: bfloat16 [4, 3072, 1152], P('dp', 'seq'), may hold values from -9 to 9
- time_embed: bfloat16 [4, 6, 1152], P('dp'), may hold values from -3 to 3
- text_tokens: bfloat16 [4, 120, 1152], P('dp'), may hold values from -9 to 9
- cotangent: bfloat16 [4, 3072, 1152], P('dp', 'seq'), may hold values from -9 to 9
- w_attn: float32 [8, 1152, 1152], P(None, 'seq', 'dp'), may hold values from -0.70710678 to 0.70710678
- w_mlp: float32 [2, 1152, 4608], P(None, 'seq', 'dp'), may hold values from -0.176776695 to 0.176776695
- bias_table: float32 [17, 1152], P(None, 'seq'), may hold values from -0.3 to 0.3
- attn_first: float32 [8, 1152, 1152], P(None, 'seq', 'dp'), may hold values from -0.0003 to 0.0003
- attn_second: float32 [8, 1152, 1152], P(None, 'seq', 'dp'), may hold values from 2.5e-09 to 1e-08
- mlp_first: float32 [2, 1152, 4608], P(None, 'seq', 'dp'), may hold values from -0.0018 to 0.0018
- mlp_second: float32 [2, 1152, 4608], P(None, 'seq', 'dp'), may hold values from 9e-08 to 3.6e-07
- table_first: float32 [17, 1152], P(None, 'seq'), may hold values from -0.0036 to 0.0036
- table_second: float32 [17, 1152], P(None, 'seq'), may hold values from 3.6e-07 to 1.4e-06
Outputs:
- block_out: bfloat16 [4, 3072, 1152], P('dp', 'seq')
- grad_latents: float32 [4, 3072, 1152], P('dp', 'seq')
- grad_time: float32 [4, 6, 1152], P('dp')
- grad_text: float32 [4, 120, 1152], P('dp')
- grad_norm: float32 [], replicated
- attn_new: float32 [8, 1152, 1152], P(None, 'seq', 'dp')
- attn_copy: bfloat16 [8, 1152, 1152], P(None, 'seq', 'dp')
- attn_first_new: float32 [8, 1152, 1152], P(None, 'seq', 'dp')
- attn_second_new: float32 [8, 1152, 1152], P(None, 'seq', 'dp')
- mlp_new: float32 [2, 1152, 4608], P(None, 'seq', 'dp')
- mlp_copy: bfloat16 [2, 1152, 4608], P(None, 'seq', 'dp')
- mlp_first_new: float32 [2, 1152, 4608], P(None, 'seq', 'dp')
- mlp_second_new: float32 [2, 1152, 4608], P(None, 'seq', 'dp')
- table_new: float32 [17, 1152], P(None, 'seq')
- table_copy: bfloat16 [17, 1152], P(None, 'seq')
- table_first_new: float32 [17, 1152], P(None, 'seq')
- table_second_new: float32 [17, 1152], P(None, 'seq')
- down_bias_grad: float32 [1152], P('seq')
All inputs are finite; a program needn't handle non-finite values.
Results may differ from a plain program's by a relative error of at most 0.015.
Values may be sent and summed in bfloat16 or wider, within the bound.
A program may use at most 384 MiB of HBM per device.

v0:
```python
import jax
import jax.numpy as jnp
from jax import lax
from jax.sharding import PartitionSpec as P

D = 1152
HEADS = 16
STEP = 10


norm_eps = 1e-06
clip_norm = 1.0
learn_rate = 0.02
first_decay = 0.5
second_decay = 0.5
adam_eps = 1e-08
weight_decay = 0.01


def layer_norm(tokens_in):
    center = tokens_in - jnp.mean(tokens_in, axis=-1, keepdims=True)
    spread = jnp.mean(center * center, axis=-1, keepdims=True)
    return center * lax.rsqrt(spread + norm_eps)


def modulate(tokens_in, shift_row, scale_row):
    return layer_norm(tokens_in) * (1.0 + scale_row) + shift_row


def gelu_tanh(pre_act):
    return jax.nn.gelu(pre_act, approximate=True)


def adam_step(weight, gradient, first_moment, second_moment, factor):
    clipped = gradient * factor
    first_new = first_decay * first_moment + (1.0 - first_decay) * clipped
    second_new = second_decay * second_moment + (1.0 - second_decay) * clipped * clipped
    first_hat = first_new / (1.0 - first_decay**STEP)
    second_hat = second_new / (1.0 - second_decay**STEP)
    updated = weight - learn_rate * (
        first_hat / (jnp.sqrt(second_hat) + adam_eps) + weight_decay * weight
    )
    return (updated, first_new, second_new)


def column_sum(matrix):
    return jnp.sum(matrix.astype(jnp.float32), axis=0)


def over_seq(partials):
    return (
        lax.psum_scatter(partials[0], "seq", scatter_dimension=1, tiled=True),
        lax.psum_scatter(partials[1], "seq", scatter_dimension=1, tiled=True),
        lax.psum_scatter(partials[2], "seq", scatter_dimension=1, tiled=True),
    )


def over_dp(partials):
    matrices = (
        lax.psum_scatter(partials[0], "dp", scatter_dimension=2, tiled=True),
        lax.psum_scatter(partials[1], "dp", scatter_dimension=2, tiled=True),
    )
    vec_sum = lax.psum(partials[2], "dp")
    return (matrices[0], matrices[1], vec_sum)


def body(
    latents,
    time_embed,
    text_tokens,
    cotangent,
    w_attn,
    w_mlp,
    bias_table,
    attn_first,
    attn_second,
    mlp_first,
    mlp_second,
    table_first,
    table_second,
):
    f32 = jnp.float32
    bf16 = jnp.bfloat16
    seq_count = lax.axis_size("seq")
    head_dim = D // HEADS
    score_scale = head_dim ** (-0.5)
    tokens_in = latents[0].astype(f32)
    seq_rows = tokens_in.shape[0]
    text_rows = text_tokens[0]
    text_count = text_rows.shape[0]
    grad_out = cotangent[0].astype(f32)
    wide_parts = (
        lax.all_gather(w_attn.astype(bf16), "dp", axis=2, tiled=True),
        lax.all_gather(w_mlp.astype(bf16), "dp", axis=2, tiled=True),
    )
    attn_w, mlp_w, table_low = (
        lax.all_gather(wide_parts[0], "seq", axis=1, tiled=True),
        lax.all_gather(wide_parts[1], "seq", axis=1, tiled=True),
        lax.all_gather(bias_table.astype(bf16), "seq", axis=1, tiled=True),
    )
    biases = table_low.astype(f32)
    modulation = biases[0:6] + time_embed[0].astype(f32)
    act_in = modulate(tokens_in, modulation[0], modulation[1]).astype(bf16)
    qkv_bias = jnp.stack([biases[6], jnp.zeros_like(biases[6]), biases[7]])
    qkv_rows = (
        jnp.einsum("sd,jde->sje", act_in, attn_w[0:3], preferred_element_type=f32) + qkv_bias
    ).astype(bf16)
    heads_in = lax.all_to_all(qkv_rows, "seq", split_axis=2, concat_axis=0, tiled=True)
    seq_len = heads_in.shape[0]
    local_heads = heads_in.shape[2] // head_dim
    block_rows = min(512, seq_len)
    block_count = seq_len // block_rows
    queries = heads_in[:, 0].reshape(seq_len, local_heads, head_dim)
    key_heads = heads_in[:, 1].reshape(seq_len, local_heads, head_dim)
    value_heads = heads_in[:, 2].reshape(seq_len, local_heads, head_dim)
    query_blocks = queries.reshape(block_count, block_rows, local_heads, head_dim)

    def forward_block(query_block):
        scores = (
            jnp.einsum("qhc,khc->hqk", query_block, key_heads, preferred_element_type=f32)
            * score_scale
        )
        row_peak = jnp.max(scores, axis=-1, keepdims=True)
        exponent = jnp.exp(scores - row_peak)
        row_total = jnp.sum(exponent, axis=-1, keepdims=True)
        prob_low = (exponent / row_total).astype(bf16)
        mixed_out = jnp.einsum("hqk,khc->qhc", prob_low, value_heads, preferred_element_type=f32)
        return (mixed_out, (row_peak + jnp.log(row_total))[..., 0])

    mixed_out, log_total = lax.map(forward_block, query_blocks)
    head_out = mixed_out.reshape(seq_len, local_heads * head_dim).astype(bf16)
    attended = lax.all_to_all(head_out, "seq", split_axis=0, concat_axis=1, tiled=True)
    branch = jnp.dot(attended, attn_w[3], preferred_element_type=f32) + biases[8]
    first_sum = tokens_in + modulation[2] * branch
    cross_in = first_sum.astype(bf16)
    cross_q = (jnp.dot(cross_in, attn_w[4], preferred_element_type=f32) + biases[9]).astype(bf16)
    text_k = jnp.dot(text_rows, attn_w[5], preferred_element_type=f32).astype(bf16)
    text_v = (jnp.dot(text_rows, attn_w[6], preferred_element_type=f32) + biases[10]).astype(bf16)
    query_three = cross_q.reshape(seq_rows, HEADS, head_dim)
    key_three = text_k.reshape(text_count, HEADS, head_dim)
    value_three = text_v.reshape(text_count, HEADS, head_dim)
    cross_scores = (
        jnp.einsum("shc,thc->hst", query_three, key_three, preferred_element_type=f32) * score_scale
    )
    cross_probs = jax.nn.softmax(cross_scores, axis=-1)
    cross_low = cross_probs.astype(bf16)
    cross_out = (
        jnp.einsum("hst,thc->shc", cross_low, value_three, preferred_element_type=f32)
        .reshape(seq_rows, D)
        .astype(bf16)
    )
    cross_branch = jnp.dot(cross_out, attn_w[7], preferred_element_type=f32) + biases[11]
    second_sum = first_sum + cross_branch
    act_mid = modulate(second_sum, modulation[3], modulation[4]).astype(bf16)
    hidden_pre = jnp.dot(act_mid, mlp_w[0], preferred_element_type=f32) + biases[13:17].reshape(-1)
    hidden = gelu_tanh(hidden_pre).astype(bf16)
    mlp_branch = jnp.einsum("sf,df->sd", hidden, mlp_w[1], preferred_element_type=f32) + biases[12]
    result = second_sum + modulation[5] * mlp_branch
    grad_mlp_branch = (modulation[5] * grad_out).astype(bf16)
    gate_mlp = jnp.sum(grad_out * mlp_branch, axis=0)
    grad_hidden = jnp.einsum("sd,df->sf", grad_mlp_branch, mlp_w[1], preferred_element_type=f32)
    grad_down = jnp.einsum("sd,sf->df", grad_mlp_branch, hidden, preferred_element_type=f32)
    _, gelu_back = jax.vjp(gelu_tanh, hidden_pre)
    grad_pre = gelu_back(grad_hidden)[0].astype(bf16)
    grad_up = jnp.einsum("sd,sf->df", act_mid, grad_pre, preferred_element_type=f32)
    grad_act_mid = jnp.einsum("sf,df->sd", grad_pre, mlp_w[0], preferred_element_type=f32)
    _, norm_back_mid = jax.vjp(modulate, second_sum, modulation[3], modulation[4])
    grad_second, shift_mid, scale_mid = norm_back_mid(grad_act_mid)
    grad_second = grad_out + grad_second
    grad_cross_branch = grad_second.astype(bf16)
    grad_cross_proj = jnp.einsum(
        "sd,se->de", cross_out, grad_cross_branch, preferred_element_type=f32
    )
    grad_cross_out = jnp.einsum(
        "se,de->sd", grad_cross_branch, attn_w[7], preferred_element_type=f32
    ).astype(bf16)
    grad_cross_three = grad_cross_out.reshape(seq_rows, HEADS, head_dim)
    grad_probs = jnp.einsum(
        "shc,thc->hst", grad_cross_three, value_three, preferred_element_type=f32
    )
    grad_cross_scores = (
        cross_probs * (grad_probs - jnp.sum(grad_probs * cross_probs, axis=-1, keepdims=True))
    ).astype(bf16)
    grad_cross_q = (
        (
            jnp.einsum("hst,thc->shc", grad_cross_scores, key_three, preferred_element_type=f32)
            * score_scale
        )
        .reshape(seq_rows, D)
        .astype(bf16)
    )
    part_k = (
        jnp.einsum(
            "hst,shc->thc", grad_cross_scores, query_three, preferred_element_type=f32
        ).reshape(text_count, D)
        * score_scale
    )
    part_v = jnp.einsum(
        "hst,shc->thc", cross_low, grad_cross_three, preferred_element_type=f32
    ).reshape(text_count, D)
    grad_cq_w = jnp.einsum("sd,se->de", cross_in, grad_cross_q, preferred_element_type=f32)
    grad_first = grad_second + jnp.einsum(
        "se,de->sd", grad_cross_q, attn_w[4], preferred_element_type=f32
    )
    grad_branch = (modulation[2] * grad_first).astype(bf16)
    gate_attn = jnp.sum(grad_first * branch, axis=0)
    grad_proj = jnp.einsum("sd,se->de", attended, grad_branch, preferred_element_type=f32)
    grad_attended = jnp.einsum(
        "se,de->sd", grad_branch, attn_w[3], preferred_element_type=f32
    ).astype(bf16)
    grad_heads = lax.all_to_all(grad_attended, "seq", split_axis=1, concat_axis=0, tiled=True)
    grad_blocks = grad_heads.reshape(block_count, block_rows, local_heads, head_dim)

    def backward_block(running, block_in):
        grad_keys, grad_values = running
        query_block, grad_block, log_block = block_in
        scores = (
            jnp.einsum("qhc,khc->hqk", query_block, key_heads, preferred_element_type=f32)
            * score_scale
        )
        prob_rows = jnp.exp(scores - log_block[..., None])
        grad_prob = jnp.einsum("qhc,khc->hqk", grad_block, value_heads, preferred_element_type=f32)
        grad_scores = (
            prob_rows * (grad_prob - jnp.sum(grad_prob * prob_rows, axis=-1, keepdims=True))
        ).astype(bf16)
        grad_query = (
            jnp.einsum("hqk,khc->qhc", grad_scores, key_heads, preferred_element_type=f32)
            * score_scale
        )
        grad_keys = (
            grad_keys
            + jnp.einsum("hqk,qhc->khc", grad_scores, query_block, preferred_element_type=f32)
            * score_scale
        )
        grad_values = grad_values + jnp.einsum(
            "hqk,qhc->khc", prob_rows.astype(bf16), grad_block, preferred_element_type=f32
        )
        return ((grad_keys, grad_values), grad_query.astype(bf16))

    empty_heads = jnp.zeros((seq_len, local_heads, head_dim), f32)
    (grad_keys, grad_values), grad_queries = lax.scan(
        backward_block, (empty_heads, empty_heads), (query_blocks, grad_blocks, log_total)
    )
    grad_head_rows = jnp.stack(
        [
            grad_queries.reshape(seq_len, -1),
            grad_keys.reshape(seq_len, -1).astype(bf16),
            grad_values.reshape(seq_len, -1).astype(bf16),
        ],
        axis=1,
    )
    grad_qkv = lax.all_to_all(grad_head_rows, "seq", split_axis=0, concat_axis=2, tiled=True)
    grad_qkv_w = jnp.einsum("sd,sje->jde", act_in, grad_qkv, preferred_element_type=f32)
    grad_act_in = jnp.einsum("sje,jde->sd", grad_qkv, attn_w[0:3], preferred_element_type=f32)
    _, norm_back_in = jax.vjp(modulate, tokens_in, modulation[0], modulation[1])
    grad_tokens, shift_in, scale_in = norm_back_in(grad_act_in)
    grad_tokens = grad_first + grad_tokens
    mod_part = jnp.stack([shift_in, scale_in, gate_attn, shift_mid, scale_mid, gate_mlp])
    grad_time, grad_text_k, grad_text_v = lax.psum((mod_part, part_k, part_v), "seq")
    text_k_low = grad_text_k.astype(bf16)
    text_v_low = grad_text_v.astype(bf16)
    grad_words = jnp.einsum(
        "te,de->td", text_k_low, attn_w[5], preferred_element_type=f32
    ) + jnp.einsum("te,de->td", text_v_low, attn_w[6], preferred_element_type=f32)
    slice_width = D // seq_count
    own_cols = jnp.arange(D) // slice_width == lax.axis_index("seq")
    own_words = jnp.where(own_cols[None, :], text_rows, jnp.zeros_like(text_rows))
    grad_k_w = jnp.einsum("td,te->de", own_words, text_k_low, preferred_element_type=f32)
    grad_v_w = jnp.einsum("td,te->de", own_words, text_v_low, preferred_element_type=f32)
    bias_text_v = jnp.where(own_cols, column_sum(text_v_low), 0.0)
    grad_attn = jnp.concatenate(
        [grad_qkv_w, jnp.stack([grad_proj, grad_cq_w, grad_k_w, grad_v_w, grad_cross_proj])], axis=0
    )
    grad_mlp = jnp.stack([grad_up, grad_down])
    bias_rows = jnp.stack(
        [
            column_sum(grad_qkv[:, 0]),
            column_sum(grad_qkv[:, 2]),
            column_sum(grad_branch),
            column_sum(grad_cross_q),
            bias_text_v,
            column_sum(grad_cross_branch),
            column_sum(grad_mlp_branch),
        ]
    )
    grad_table = jnp.concatenate([mod_part, bias_rows, column_sum(grad_pre).reshape(4, D)], axis=0)
    partials = (grad_attn, grad_mlp, grad_table)
    reduced = over_dp(over_seq(partials))
    own_attn, own_mlp, own_table = reduced
    table_square = jnp.where(lax.axis_index("dp") == 0, jnp.sum(own_table * own_table), 0.0)
    square_total = lax.psum(
        jnp.sum(own_attn * own_attn) + jnp.sum(own_mlp * own_mlp) + table_square, ("dp", "seq")
    )
    grad_norm = jnp.sqrt(square_total)
    factor = jnp.minimum(1.0, clip_norm / (grad_norm + 1e-06))
    attn_new, attn_first_new, attn_second_new = adam_step(
        w_attn, own_attn, attn_first, attn_second, factor
    )
    mlp_new, mlp_first_new, mlp_second_new = adam_step(
        w_mlp, own_mlp, mlp_first, mlp_second, factor
    )
    table_new, table_first_new, table_second_new = adam_step(
        bias_table, own_table, table_first, table_second, factor
    )
    return (
        result.astype(bf16)[None],
        grad_tokens[None],
        grad_time[None],
        grad_words[None],
        grad_norm,
        attn_new,
        attn_new.astype(bf16),
        attn_first_new,
        attn_second_new,
        mlp_new,
        mlp_new.astype(bf16),
        mlp_first_new,
        mlp_second_new,
        table_new,
        table_new.astype(bf16),
        table_first_new,
        table_second_new,
        own_table[12],
    )


def solution(mesh):
    return jax.shard_map(
        body,
        mesh=mesh,
        in_specs=(
            P("dp", "seq", None),
            P("dp", None, None),
            P("dp", None, None),
            P("dp", "seq", None),
            P(None, "seq", "dp"),
            P(None, "seq", "dp"),
            P(None, "seq"),
            P(None, "seq", "dp"),
            P(None, "seq", "dp"),
            P(None, "seq", "dp"),
            P(None, "seq", "dp"),
            P(None, "seq"),
            P(None, "seq"),
        ),
        out_specs=(
            P("dp", "seq", None),
            P("dp", "seq", None),
            P("dp", None, None),
            P("dp", None, None),
            P(),
            P(None, "seq", "dp"),
            P(None, "seq", "dp"),
            P(None, "seq", "dp"),
            P(None, "seq", "dp"),
            P(None, "seq", "dp"),
            P(None, "seq", "dp"),
            P(None, "seq", "dp"),
            P(None, "seq", "dp"),
            P(None, "seq"),
            P(None, "seq"),
            P(None, "seq"),
            P(None, "seq"),
            P("seq"),
        ),
        check_vma=False,
    )
```

profile of v0, /device:TPU:0, one launch (start us, length us, event | category | flops | bytes accessed | tf_op | source)
XLA Modules:
  0.0 1920.5 jit_solution(3790885396561971291)
XLA Ops:
  11.8 58.9 %all-gather.6.cloned.1.call-done = bf16[8,144,1152]{1,0,2:T(8,128)(2,1)} async-done(((bf16[8,144,288]{1,0,2:T(8,128)(2,1)}), bf16[8,144,1152]{1,0,2:T(8,128)(2,1)}) %all-gather.6.cloned.1.call-update) | async-done | bytes 2654224 | tf_op jit(solution)/shard_map/all_gather | solution.py:93
  77.5 35.5 %all-gather.10.cloned.1.call-done = bf16[2,144,4608]{2,1,0:T(8,128)(2,1)} async-done(((bf16[2,144,1152]{2,1,0:T(8,128)(2,1)}), bf16[2,144,4608]{2,1,0:T(8,128)(2,1)}) %all-gather.10.cloned.1.call-update) | async-done | bytes 2654224 | tf_op jit(solution)/shard_map/all_gather | solution.py:94
  113.1 14.0 all-gather
  129.2 173.1 %all-gather.8.cloned.1.call-done = bf16[8,1152,1152]{2,1,0:T(8,128)(2,1)} async-done(((bf16[8,144,1152]{2,1,0:T(8,128)(2,1)}), bf16[8,1152,1152]{2,1,0:T(8,128)(2,1)}) %all-gather.8.cloned.1.call-update) | async-done | bytes 21233680 | tf_op jit(solution)/shard_map/all_gather | solution.py:97
  323.3 175.2 %all-to-all-done = bf16[384,3,1152]{0,1,2:T(4,128)(2,1)} async-done(((bf16[384,3,1152]{0,1,2:T(4,128)(2,1)}), bf16[384,3,1152]{0,1,2:T(4,128)(2,1)}, u32[]{:S(2)}, u32[]{:S(2)}) %all-to-all-start) | async-done | bytes 2654240 | tf_op jit(solution)/shard_map/all_to_all | solution.py:108
  505.2 51.3 %while.27 = (s32[]{:T(128)}, bf16[6,512,2,72]{1,3,2,0:T(8,128)(2,1)}, f32[6,2,512]{2,1,0:T(2,128)}, bf16[6,512,2,72]{1,3,2,0:T(8,128)(2,1)S(1)}, bf16[3072,2,72]...) while((s32[]{:T(128)}, bf16[6,512,2,72]{1,3,2,0:T(8,128)(2,1)}, ...), condition=%wide.region_5.6_spmd, body=%wide.region_2.5_spmd.sunk | while | flops 934280192 | bytes 39993440 | solution.py:130
  575.3 15.7 all-to-all-done.1
  633.7 12.4 convert_reduce_fusion
  656.5 23.0 %pad_maximum_fusion = f32[2,1152,4608]{2,1,0:T(8,128)} fusion(f32[1,1152,4608]{2,1,0:T(8,128)S(1)} %bitcast.343, f32[1,1152,4608]{2,1,0:T(8,128)} %convolution_bitcast_fusion.1), kind=kLoop, calls=%fused_computation.46 | loop fusion | flops 10616832 | bytes 84934656 | tf_op jit(solution)/shard_map/stack | solution.py:274
  680.3 12.7 multiply_reduce_fusion.5
  693.0 13.6 convert_reduce_fusion.2
  734.9 37.5 %all-to-all-done.2 = bf16[384,8,144]{0,2,1:T(8,128)(2,1)S(1)} async-done(((bf16[384,8,144]{0,2,1:T(8,128)(2,1)}), bf16[384,8,144]{0,2,1:T(8,128)(2,1)S(1)}, u32[]{:S(2)}, u32[]{:S(2)}) %all-to-all-start.2) | async-done | bytes 884768 | tf_op jit(solution)/shard_map/all_to_all | solution.py:211
  780.5 163.6 %while.28 = (s32[]{:T(128)}, f32[3072,2,72]{0,2,1:T(8,128)S(1)}, f32[3072,2,72]{0,2,1:T(8,128)}, bf16[6,512,2,72]{1,3,2,0:T(8,128)(2,1)}, bf16[6,512,2,72]{1,3,2...) while((s32[]{:T(128)}, f32[3072,2,72]{0,2,1:T(8,128)S(1)}, ...), condition=%wide.region_15.16_spmd.clone, body=%wide.region_13.15_spmd.clone.sunk | while | flops 2305031168 | bytes 119025872 | solution.py:241
  980.5 102.5 %all-to-all-done.3 = bf16[8,2,82944]{2,1,0:T(2,128)(2,1)S(1)} async-done(((bf16[8,2,82944]{2,1,0:T(2,128)(2,1)}), bf16[8,2,82944]{2,1,0:T(2,128)(2,1)S(1)}, u32[]{:S(2)}, u32[]{:S(2)}) %all-to-all-start.3) | async-done | bytes 2654240 | tf_op jit(solution)/shard_map/all_to_all | solution.py:252
  1114.7 71.8 %all-reduce.2 = (f32[1,6,1152]{2,1,0:T(8,128)}, bf16[120,1152]{0,1:T(8,128)(2,1)}, bf16[120,1152]{0,1:T(8,128)(2,1)}) all-reduce(f32[1,6,1152]{2,1,0:T(8,128)} %bitcast.374, f32[120,1152]{0,1:T(8,128)} %bitcast.361, f32[120,1152]{0,1:T(8,128)} %bitcast.368), channel_id=1, replica_groups=mesh['dp'=4,'seq'=8] {'seq'}, use_global_device_ids=true, to_apply=%region_24.25 | all-reduce | flops 283392 | bytes 1714176 | tf_op jit(solution)/shard_map/psum | solution.py:259
  1213.8 43.4 %copy.223 = f32[8,1152,1152]{2,0,1:T(8,128)} copy(f32[8,1152,1152]{1,2,0:T(8,128)} %fusion.47) | data formatting | bytes 84934656 | tf_op jit(solution)/shard_map/concatenate | solution.py:271
  1261.0 404.0 %reduce-scatter.10.cloned.1.call-done = f32[8,144,1152]{2,0,1:T(8,128)} async-done(((f32[8,1152,1152]{2,0,1:T(8,128)}), f32[8,144,1152]{2,0,1:T(8,128)}) %reduce-scatter.10.cloned.1.call-update) | async-done | bytes 5308432 | tf_op jit(solution)/shard_map/reduce_scatter | solution.py:52
  1664.9 43.6 %copy.241 = f32[8,144,1152]{0,1,2:T(8,128)} copy(f32[8,144,1152]{2,0,1:T(8,128)} %reduce-scatter.10.cloned.1.call-done) | data formatting | bytes 10616832
  1708.5 56.9 %reshape.307 = f32[1152,1152]{1,0:T(8,128)} reshape(f32[1152,144,8]{2,1,0:T(8,128)} %bitcast.74) | data formatting | bytes 10616832
  1774.7 16.9 psum.38
  1795.1 31.3 %reduce-scatter.16.cloned.1.call-done = f32[288,1152]{1,0:T(8,128)} async-done(((f32[1152,1152]{1,0:T(8,128)}), f32[288,1152]{1,0:T(8,128)}) %reduce-scatter.16.cloned.1.call-update) | async-done | bytes 1327120
  1826.5 14.3 reshape.308
  1840.8 14.0 copy.242
  1858.5 39.3 %psum.39 = f32[]{:T(128)} all-reduce(f32[]{:T(128)S(6)} %add.313), channel_id=1, replica_groups=mesh['dp'=4,'seq'=8] {'dp','seq'}, use_global_device_ids=true, to_apply=%region_44.45 | all-reduce | flops 1 | bytes 8 | tf_op jit(solution)/shard_map/psum | solution.py:291
  (442 shorter events, 491.2 us)
Async XLA Ops:
  7.2 63.5 %all-gather.6.cloned.1.call-start = ((), (), s32[]{:S(2)}) async-start(), calls=%async_computation.9 | async-start | bytes 5898240 | tf_op jit(solution)/shard_map/all_gather | solution.py:93
  10.7 102.3 %all-gather.10.cloned.1.call-start = ((), (), s32[]{:S(2)}) async-start(), calls=%async_computation.11 | async-start | bytes 3317760 | tf_op jit(solution)/shard_map/all_gather | solution.py:94
  11.7 290.6 %all-gather.8.cloned.1.call-start = ((), (), s32[]{:S(2)}) async-start(), calls=%async_computation.10 | async-start | bytes 23887872 | tf_op jit(solution)/shard_map/all_gather | solution.py:97
  77.4 35.6 %copy-start.63 = (f32[17,144]{1,0:T(8,128)S(1)}, f32[17,144]{1,0:T(8,128)}, u32[]{:S(2)}) copy-start(f32[17,144]{1,0:T(8,128)} %param.23) | copy-start | bytes 29380
  77.4 49.8 %copy-start.3 = (bf16[1,384,1152]{2,1,0:T(8,128)(2,1)S(1)}, bf16[1,384,1152]{2,1,0:T(8,128)(2,1)}, u32[]{:S(2)}) copy-start(bf16[1,384,1152]{2,1,0:T(8,128)(2,1)} %param.17) | copy-start | bytes 2654212
  77.5 50.9 %copy-start.90 = (bf16[1,6,1152]{2,1,0:T(8,128)(2,1)S(1)}, bf16[1,6,1152]{2,1,0:T(8,128)(2,1)}, u32[]{:S(2)}) copy-start(bf16[1,6,1152]{2,1,0:T(8,128)(2,1)} %param.18) | copy-start | bytes 41476
  77.5 535.2 %all-gather.12.cloned.1.call-start = ((), (), s32[]{:S(2)}) async-start(), calls=%async_computation.12 | async-start | bytes 23887872 | tf_op jit(solution)/shard_map/all_gather | solution.py:98
  127.3 183.7 %copy-start.47 = (f32[1152,17]{0,1:T(8,128)}, f32[1152,17]{0,1:T(8,128)S(1)}, u32[]{:S(2)}) copy-start(f32[1152,17]{0,1:T(8,128)S(1)} %reshape.303) | copy-start | bytes 235012
  127.5 183.5 %copy-start.67 = (f32[384]{0:T(512)}, f32[384]{0:T(512)S(1)}, u32[]{:S(2)}) copy-start(f32[384]{0:T(512)S(1)} %broadcast_multiply_fusion.1) | copy-start | bytes 4612
  127.9 183.1 %copy-start.79 = (f32[384]{0:T(512)}, f32[384]{0:T(512)S(1)}, u32[]{:S(2)}) copy-start(f32[384]{0:T(512)S(1)} %fusion.140) | copy-start | bytes 4612
  129.2 181.8 %copy-start.54 = (f32[1152]{0:T(1024)}, f32[1152]{0:T(1024)S(1)}, u32[]{:S(2)}) copy-start(f32[1152]{0:T(1024)S(1)} %get-tuple-element.421) | copy-start | bytes 13828
  129.2 181.8 %copy-start.76 = (f32[1152]{0:T(1024)}, f32[1152]{0:T(1024)S(1)}, u32[]{:S(2)}) copy-start(f32[1152]{0:T(1024)S(1)} %get-tuple-element.422) | copy-start | bytes 13828
  318.6 180.0 %all-to-all-start = ((bf16[384,3,1152]{0,1,2:T(4,128)(2,1)}), bf16[384,3,1152]{0,1,2:T(4,128)(2,1)}, u32[]{:S(2)}, u32[]{:S(2)}) async-start(bf16[384,3,1152]{0,1,2:T(4,128)(2,1)} %copy.199), calls=%async_computation | async-start | bytes 7077888 | tf_op jit(solution)/shard_map/all_to_all | solution.py:108
  564.4 26.6 %all-to-all-start.1 = ((bf16[8,384,144]{1,2,0:T(8,128)(2,1)}), bf16[8,384,144]{1,2,0:T(8,128)(2,1)S(1)}, u32[]{:S(2)}, u32[]{:S(2)}) async-start(bf16[8,384,144]{1,2,0:T(8,128)(2,1)} %copy.204), calls=%async_computation.1 | async-start | bytes 1769472 | tf_op jit(solution)/shard_map/all_to_all | solution.py:132
  568.0 692.3 %reduce-scatter.12.cloned.1.call-start = ((), (), s32[]{:S(2)}) async-start(), calls=%async_computation.14 | async-start | bytes 47775744 | tf_op jit(solution)/shard_map/reduce_scatter | solution.py:53
  572.6 32.9 %copy-start.49 = (bf16[120,1152]{0,1:T(8,128)(2,1)}, bf16[120,1152]{0,1:T(8,128)(2,1)S(1)}, u32[]{:S(2)}) copy-start(bf16[120,1152]{0,1:T(8,128)(2,1)S(1)} %copy.205) | copy-start | bytes 829444
  730.9 41.5 %all-to-all-start.2 = ((bf16[384,8,144]{0,2,1:T(8,128)(2,1)}), bf16[384,8,144]{0,2,1:T(8,128)(2,1)S(1)}, u32[]{:S(2)}, u32[]{:S(2)}) async-start(bf16[384,8,144]{0,2,1:T(8,128)(2,1)} %bitcast.35), calls=%async_computation.2 | async-start | bytes 1769472 | tf_op jit(solution)/shard_map/all_to_all | solution.py:211
  968.4 114.6 %all-to-all-start.3 = ((bf16[8,2,82944]{2,1,0:T(2,128)(2,1)}), bf16[8,2,82944]{2,1,0:T(2,128)(2,1)S(1)}, u32[]{:S(2)}, u32[]{:S(2)}) async-start(bf16[8,2,82944]{2,1,0:T(2,128)(2,1)} %reshape.322), calls=%async_computation.3 | async-start | bytes 5308416 | tf_op jit(solution)/shard_map/all_to_all | solution.py:252
  972.2 692.7 %reduce-scatter.10.cloned.1.call-start = ((), (), s32[]{:S(2)}) async-start(), calls=%async_computation.13 | async-start | bytes 47775744 | tf_op jit(solution)/shard_map/reduce_scatter | solution.py:52
  1257.3 516.4 %reduce-scatter.18.cloned.1.call-start = ((), (), s32[]{:S(2)}) async-start(), calls=%async_computation.17 | async-start | bytes 663552
  1260.2 532.7 %reduce-scatter.14.cloned.1.call-start = ((), (), s32[]{:S(2)}) async-start(), calls=%async_computation.15 | async-start | bytes 6635520 | tf_op jit(solution)/shard_map/reduce_scatter | solution.py:61
  1260.9 565.6 %reduce-scatter.16.cloned.1.call-start = ((), (), s32[]{:S(2)}) async-start(), calls=%async_computation.16 | async-start | bytes 6635520
  1791.6 49.3 %copy-start.52 = (f32[17,144]{1,0:T(8,128)}, f32[17,144]{1,0:T(8,128)S(1)}, u32[]{:S(2)}) copy-start(f32[17,144]{1,0:T(8,128)S(1)} %psum.38) | copy-start | bytes 29380
  1854.8 43.7 %copy-start.14 = (f32[8,144,288]{2,1,0:T(8,128)S(1)}, f32[8,144,288]{2,1,0:T(8,128)}, u32[]{:S(2)}) copy-start(f32[8,144,288]{2,1,0:T(8,128)} %param.21) | copy-start | bytes 3981316
  (104 other events, 603.5 us)
Sparse Core Ops, SparseCore 0:
  10.9 59.7 all-gather.5
  73.1 39.9 all-gather.9
  114.7 187.6 all-gather.7
  303.8 261.3 all-gather.11
  679.7 481.7 reduce-scatter.11
  1257.5 407.4 reduce-scatter.9
  1667.8 29.4 reduce-scatter.17
  1700.3 60.1 reduce-scatter.13
  1765.5 60.9 reduce-scatter.15
where the time goes:
time: 1930 us; the launch traced here: 1920 us
  waiting for transfers between devices  1030 us (53%)
  matrix products  311 us (16%)
  local copies, waits for them, and re-layouts  290 us (15%)
  blocking collectives  142 us (7%)
  other arithmetic  106 us (5%)
    reduce_scatter x1, waiting for transfers between devices, over_seq(): lax.psum_scatter(partials[0], 'seq', scatter_dimension=1, tiled=True)  404 us
    all_to_all x1, waiting for transfers between devices, body(): lax.all_to_all(qkv_rows, 'seq', split_axis=2, concat_axis=0, tiled=True)  175 us
    unnamed x220, local copies, waits for them, and re-layouts  174 us
    all_gather x1, waiting for transfers between devices, body(): lax.all_gather(wide_parts[0], 'seq', axis=1, tiled=True)  173 us
    all_to_all x1, waiting for transfers between devices, body(): lax.all_to_all(grad_head_rows, 'seq', split_axis=0, concat_axis=2, tiled=...  102 us
    psum x1, blocking collectives, body(): lax.psum((mod_part, part_k, part_v), 'seq')  71.8 us
    all_gather x1, waiting for transfers between devices, body(): lax.all_gather(w_attn.astype(bf16), 'dp', axis=2, tiled=True)  58.9 us
    dot_general x6, matrix products, backward_block(): jnp.einsum('qhc,khc->hqk', grad_block, value_heads, preferred_element_typ...  45.3 us
  transfers between devices with their start and end apart: 13, of which 9 were waited for; matrix products, arithmetic and copies ran while one was open for 30% of the time, Pallas kernels for 0%

commit v1 on v0

v1 whole, which is shorter than its diff:
```python
import functools
import math

import jax
import jax.numpy as jnp
from jax import lax
from jax.experimental import pallas as pl
from jax.experimental.pallas import tpu as pltpu
from jax.sharding import PartitionSpec as P

STEP = 10

norm_eps = 1e-06
clip_norm = 1.0
learn_rate = 0.02
first_decay = 0.5
second_decay = 0.5
adam_eps = 1e-08
weight_decay = 0.01

HEAD_DIM = 72
MESH = pl.DeviceIdType.MESH
f32 = jnp.float32
bf16 = jnp.bfloat16
MIB = 1 << 20


class Grid:
    def __init__(self, mesh):
        self.np = mesh.shape["dp"]
        self.ns = mesh.shape["seq"]
        root = math.isqrt(self.np)
        self.ax = root if root * root == self.np else self.np
        self.ay = self.np // self.ax
        self.nc = 2 if self.ns % 2 == 0 else 1
        self.nz = self.ns // self.nc
        self.paired = self.nz & (self.nz - 1) == 0

    def here(self):
        p = lax.axis_index("dp")
        s = lax.axis_index("seq")
        return p // self.ax, p % self.ax, s // self.nc, s % self.nc

    def device(self, y, x, z, c):
        return (y * self.ax + x, z * self.nc + c)


def turn(value, step, size):
    return (value + step) % size


class Copies:
    def __init__(self, send_sem, recv_sem, me):
        self.send_sem, self.recv_sem, self.me = send_sem, recv_sem, me
        self.started = []
        self.count = 0

    def make(self, slot, into, src, dst, device):
        return pltpu.make_async_remote_copy(
            src_ref=src,
            dst_ref=dst,
            send_sem=self.send_sem.at[slot],
            recv_sem=self.recv_sem.at[into],
            device_id=device,
            device_id_type=MESH,
        )

    def reserve(self):
        self.count += 1
        return self.count - 1

    def send(self, refs, into=None, when=None):
        slot = self.reserve()
        into = slot if into is None else into
        self.started.append((slot, into, refs, when))

        def start():
            self.make(slot, into, *refs()).start()

        if when is None:
            start()
        else:
            pl.when(when())(start)
        return slot

    def arrived(self, slot, landed):
        self.make(slot, slot, landed, landed, self.me).wait_recv()

    def finish(self):
        for slot, into, refs, when in self.started:

            def done(slot=slot, into=into, refs=refs):
                self.make(slot, into, *refs()).wait_send()

            if when is None:
                done()
            else:
                pl.when(when())(done)


class Local:
    def __init__(self, sems, slot, refs):
        self.sems, self.slot, self.refs = sems, slot, refs
        pltpu.make_async_copy(*refs(), sems.at[slot]).start()

    def wait(self):
        pltpu.make_async_copy(*self.refs(), self.sems.at[self.slot]).wait()


def greet(devices):
    barrier = pltpu.get_barrier_semaphore()
    for device in devices:
        pl.semaphore_signal(barrier, inc=1, device_id=device, device_id_type=MESH)
    pl.semaphore_wait(barrier, len(devices))


def partners(grid, y, x, z, c):
    p, s = grid.device(y, x, z, c)
    found = [(p, turn(s, r, grid.ns)) for r in range(1, grid.ns)]
    found += [(turn(p, r, grid.np), s) for r in range(1, grid.np)]
    return found


def flip_bits(value, r):
    out, bit = value, 1
    while bit <= r:
        if r & bit:
            out = out + bit * (1 - 2 * ((value // bit) % 2))
        bit *= 2
    return out


class Site:
    def __init__(self, grid, send_sem, recv_sem, local_sem):
        self.grid = grid
        self.y, self.x, self.z, self.c = grid.here()
        self.p, self.s = grid.device(self.y, self.x, self.z, self.c)
        self.copies = Copies(send_sem, recv_sem, (self.p, self.s))
        self.local_sem = local_sem
        self.locals = 0
        greet(partners(grid, self.y, self.x, self.z, self.c))

    def local(self, refs):
        self.locals += 1
        return Local(self.local_sem, self.locals - 1, refs)

    def along(self, first_x, r, second=False):
        g = self.grid
        if first_x != second:
            return g.device(self.y, turn(self.x, r, g.ax), self.z, self.c)
        return g.device(turn(self.y, r, g.ay), self.x, self.z, self.c)

    def z_to(self, r):
        return flip_bits(self.z, r) if self.grid.paired else turn(self.z, r, self.grid.nz)

    def z_from(self, r):
        return flip_bits(self.z, r) if self.grid.paired else turn(self.z, self.grid.nz - r, self.grid.nz)

    def z_device(self, r):
        return self.grid.device(self.y, self.x, self.z_to(r), self.c)

    def other_core(self):
        return self.grid.device(self.y, self.x, self.z, 1 - self.c)


def pieces_of(rows, i):
    cut = (rows // 2 + 15) // 16 * 16
    if rows % 16 == 0 and cut < rows:
        return [(0, cut, True), (cut, rows - cut, False)]
    return [(0, rows, i % 2 == 0)]


def sequence(blocks, lead=2):
    steps = []
    for i in range(len(blocks) + 2):
        for ahead in range(lead + 1) if i == 0 else (lead,):
            if i + ahead < len(blocks):
                flow, n = blocks[i + ahead]
                steps.append(("F", i + ahead, functools.partial(flow.first, n)))
        if i < len(blocks):
            flow, n = blocks[i]
            steps.append(("S", i, functools.partial(flow.second, n)))
        if 0 <= i - 1 < len(blocks):
            flow, n = blocks[i - 1]
            steps.append(("T", i - 1, functools.partial(flow.third, n)))
    return steps


def run(steps):
    for _, _, step in steps:
        step()


class ZPhase:
    def __init__(self, site, own_ref, landing):
        self.site, self.own, self.landing = site, own_ref, landing
        self.relay = site.grid.nz == 4
        self.slots = {}

    def inner(self):
        z = self.site.z
        return z * (3 - z) // 2

    def place(self, k):
        t = self.site
        if k == 0:
            return t.z
        if not self.relay:
            return t.z_from(k)
        if k == 1:
            return flip_bits(t.z, 1)
        near = self.inner() if k == 2 else 1 - self.inner()
        return near * (3 - t.z) + (1 - near) * flip_bits(t.z, 2)

    def block(self, k):
        return self.landing(self.place(k))

    def start(self):
        t = self.site
        if not self.relay:
            for k in range(1, t.grid.nz):
                self.slots[k] = t.copies.send(
                    lambda k=k: (self.own, self.landing(t.z), t.z_device(k))
                )
            return
        self.slots[1] = t.copies.send(
            lambda: (self.own, self.landing(t.z), t.z_device(1))
        )
        self.slots[2] = t.copies.reserve()
        self.slots[3] = t.copies.reserve()
        t.copies.send(
            lambda: (self.own, self.landing(t.z), t.z_device(3)),
            self.slots[2],
            lambda: self.inner() == 1,
        )

    def pass_on(self, k):
        if not self.relay:
            return
        t = self.site
        pl.when(self.inner() == 1)(lambda: t.copies.arrived(self.slots[k], self.block(k)))
        t.copies.send(
            lambda: (self.block(k), self.block(k), t.z_device(3 if k == 1 else 1)),
            self.slots[3 if k == 1 else k],
            lambda: self.inner() == 1,
        )

    def settle(self, k):
        def wait():
            self.site.copies.arrived(self.slots[k], self.block(k))

        if self.relay:
            pl.when(self.inner() == 0)(wait)
        else:
            wait()


class GatherFlow:
    def __init__(self, site, out_ref, own_ref):
        self.site, self.out, self.own = site, out_ref, own_ref
        self.rows = out_ref.shape[4]
        self.count = site.grid.nz
        self.zone = ZPhase(site, own_ref, lambda z: self.out.at[site.y, site.x, z, site.c])
        self.slots = {}

    def mine(self, n, piece=None):
        t = self.site
        if piece is None:
            return self.out.at[t.y, t.x, self.zone.place(n), t.c]
        return self.out.at[t.y, t.x, self.zone.place(n), t.c, pl.ds(piece[0], piece[1])]

    def spot(self, n, piece, dy, dx):
        t, g = self.site, self.site.grid
        return self.out.at[
            turn(t.y, g.ay - dy, g.ay),
            turn(t.x, g.ax - dx, g.ax),
            self.zone.place(n),
            t.c,
            pl.ds(piece[0], piece[1]),
        ]

    def plane(self, n, c):
        return self.out.at[:, :, self.zone.place(n), c]

    def start(self):
        self.local = self.site.local(lambda: (self.own, self.mine(0)))

    def first(self, n):
        t, g = self.site, self.site.grid
        if n:
            self.zone.settle(n)

        def refs(piece, first_x, step):
            source = self.own.at[pl.ds(piece[0], piece[1])] if n == 0 else self.mine(n, piece)
            return source, self.mine(n, piece), t.along(first_x, step)

        for piece in pieces_of(self.rows, n):
            for first_x in (piece[2], not piece[2]):
                for step in range(1, g.ax if first_x else g.ay):
                    self.slots["a", n, piece, first_x, step] = t.copies.send(
                        functools.partial(refs, piece, first_x, step)
                    )

    def second(self, n):
        t, g = self.site, self.site.grid
        for piece in pieces_of(self.rows, n):
            first_x = piece[2]
            for step in range(1, g.ax if first_x else g.ay):
                dy, dx = (0, step) if first_x else (step, 0)
                t.copies.arrived(
                    self.slots["a", n, piece, first_x, step], self.spot(n, piece, dy, dx)
                )

                def refs(piece, dy, dx, onward):
                    block = self.spot(n, piece, dy, dx)
                    return block, block, t.along(piece[2], onward, True)

                for onward in range(1, g.ay if first_x else g.ax):
                    self.slots["b", n, piece, step, onward] = t.copies.send(
                        functools.partial(refs, piece, dy, dx, onward)
                    )

    def third(self, n):
        t, g = self.site, self.site.grid
        for piece in pieces_of(self.rows, n):
            first_x = piece[2]
            for onward in range(1, g.ay if first_x else g.ax):
                dy, dx = (onward, 0) if first_x else (0, onward)
                t.copies.arrived(
                    self.slots["a", n, piece, not first_x, onward], self.spot(n, piece, dy, dx)
                )
                for step in range(1, g.ax if first_x else g.ay):
                    dy, dx = (onward, step) if first_x else (step, onward)
                    t.copies.arrived(
                        self.slots["b", n, piece, step, onward], self.spot(n, piece, dy, dx)
                    )
        if n == 0:
            self.local.wait()
        if g.nc > 1:
            self.slots["c", n] = t.copies.send(
                lambda: (self.plane(n, t.c), self.plane(n, t.c), t.other_core())
            )

    def blocks(self):
        return [(self, n) for n in range(self.count)]

    def relays(self):
        return [
            ("P", k, functools.partial(self.zone.pass_on, k)) for k in range(1, self.count)
        ]

    def finish(self):
        t, g = self.site, self.site.grid
        if g.nc > 1:
            for n in range(self.count):
                t.copies.arrived(self.slots["c", n], self.plane(n, 1 - t.c))


def weave(steps, extra):
    found = []
    for step in steps:
        found.append(step)
        found += extra.get(step[:2], [])
    return found


def add_rows(dst, srcs, lo, count):
    chunk = max([n for n in range(16, 49, 16) if count % n == 0], default=count)
    for j in range(count // chunk):
        at = pl.ds(lo + j * chunk, chunk)
        if len(srcs) == 2 and dst.dtype == bf16:
            dst[at] = srcs[0][at] + srcs[1][at]
            continue
        total = srcs[0][at].astype(f32)
        for src in srcs[1:]:
            total = total + src[at].astype(f32)
        dst[at] = total.astype(dst.dtype)


def add_blocks(count, pick, lo, rows):
    def body(i, carry):
        dst, srcs = pick(i)
        add_rows(dst, srcs, lo, rows)
        return carry

    lax.fori_loop(0, count, body, 0)


class ScatterFlow:
    def __init__(self, site, grad_ref, out_ref, mine, half_sum, got_a, got_b, got_z, column_ref=None):
        self.site, self.grad, self.out, self.column = site, grad_ref, out_ref, column_ref
        self.mine, self.half_sum, self.got_a, self.got_b, self.got_z = mine, half_sum, got_a, got_b, got_z
        self.order = list(range(site.grid.nz))[::-1]
        self.slots = {}
        self.locals = {}
        self.base = 0
        self.then = {}
        self.rows = half_sum.shape[3]

    def zone(self, n):
        r = self.order[n]
        return self.site.z_to(r) if r else self.site.z

    def load(self, n):
        t, g = self.site, self.site.grid
        if g.nc > 1:
            self.slots["core", n] = t.copies.send(
                lambda: (
                    self.grad.at[:, :, self.zone(n), 1 - t.c],
                    self.half_sum.at[n],
                    t.other_core(),
                )
            )
        self.locals[n] = t.local(
            lambda: (self.grad.at[:, :, self.zone(n), t.c], self.mine.at[self.spot(n)])
        )

    def own_part(self, n, a, b):
        return self.mine.at[self.spot(n), a, b]

    def spot(self, n):
        return (self.base + n) % self.mine.shape[0]

    def first(self, n):
        t, g = self.site, self.site.grid
        if n in self.locals:
            self.locals[n].wait()
        if g.nc > 1:
            t.copies.arrived(self.slots["core", n], self.half_sum.at[n])

        def pick(i):
            dst = self.half_sum.at[n, i // g.ax, i % g.ax]
            return dst, [self.own_part(n, i // g.ax, i % g.ax)] + ([dst] if g.nc > 1 else [])

        add_blocks(g.ay * g.ax, pick, 0, self.rows)
        if n in self.then:
            self.then[n]()

        def refs(piece, step):
            at = pl.ds(piece[0], piece[1])
            if piece[2]:
                source = self.half_sum.at[n, :, turn(t.x, step, g.ax), at]
            else:
                source = self.half_sum.at[n, turn(t.y, step, g.ay), :, at]
            return source, self.landing(n, piece, step), t.along(piece[2], step)

        for piece in pieces_of(self.rows, n):
            for step in range(1, g.ax if piece[2] else g.ay):
                self.slots["a", n, piece, step] = t.copies.send(
                    functools.partial(refs, piece, step)
                )

    def landing(self, n, piece, step):
        g = self.site.grid
        return self.got_a.at[
            n, step - 1, pl.ds(0, g.ay if piece[2] else g.ax), pl.ds(piece[0], piece[1])
        ]

    def second(self, n):
        t, g = self.site, self.site.grid
        for piece in pieces_of(self.rows, n):
            lo, rows, first_x = piece
            at = pl.ds(lo, rows)
            count, across = (g.ax, g.ay) if first_x else (g.ay, g.ax)
            for step in range(1, count):
                t.copies.arrived(self.slots["a", n, piece, step], self.landing(n, piece, step))

            def pick(i):
                dst = self.half_sum.at[n, i, t.x] if first_x else self.half_sum.at[n, t.y, i]
                return dst, [dst] + [self.got_a.at[n, step - 1, i] for step in range(1, count)]

            add_blocks(across, pick, lo, rows)

            def refs(step, first_x=first_x, at=at):
                if first_x:
                    source = self.half_sum.at[n, turn(t.y, step, g.ay), t.x, at]
                else:
                    source = self.half_sum.at[n, t.y, turn(t.x, step, g.ax), at]
                return source, self.got_b.at[n, step - 1, at], t.along(first_x, step, True)

            for step in range(1, across):
                self.slots["b", n, piece, step] = t.copies.send(functools.partial(refs, step))

    def third(self, n):
        t, g = self.site, self.site.grid
        r = self.order[n]
        own = self.half_sum.at[n, t.y, t.x]
        into = own if self.column is None else self.column.at[r]
        for piece in pieces_of(self.rows, n):
            lo, rows, first_x = piece
            across = g.ay if first_x else g.ax
            for step in range(1, across):
                t.copies.arrived(
                    self.slots["b", n, piece, step], self.got_b.at[n, step - 1, pl.ds(lo, rows)]
                )
            add_rows(into, [own] + [self.got_b.at[n, step - 1] for step in range(1, across)], lo, rows)
        if self.column is None and r:
            self.slots["z", r] = t.copies.send(
                lambda: (self.half_sum.at[n, t.y, t.x], self.got_z.at[r - 1], t.z_device(r))
            )

    def blocks(self):
        return [(self, n) for n in range(len(self.order))]

    def finish(self):
        if self.column is not None:
            return
        t, g = self.site, self.site.grid
        for r in range(1, g.nz):
            t.copies.arrived(self.slots["z", r], self.got_z.at[r - 1])
        own = self.half_sum.at[len(self.order) - 1, t.y, t.x]
        add_rows(
            self.out, [own] + [self.got_z.at[r - 1] for r in range(1, g.nz)], 0, self.rows
        )


class NearScatterFlow(ScatterFlow):
    def load(self, n):
        t = self.site
        if t.grid.nc > 1:
            self.slots["core", n] = t.copies.send(
                lambda: (self.grad.at[n, 1 - t.c], self.half_sum.at[n], t.other_core())
            )

    def own_part(self, n, a, b):
        return self.grad.at[n, self.site.c, a, b]


class ColumnSum:
    def __init__(self, site, column_ref, out_ref, own, got_z):
        self.site, self.column, self.out, self.own, self.got_z = site, column_ref, out_ref, own, got_z
        self.rows = own.shape[0]

    def start(self):
        t = self.site
        self.local = t.local(lambda: (self.column.at[0], self.own))
        self.slots = {
            r: t.copies.send(
                lambda r=r: (self.column.at[r], self.got_z.at[r - 1], t.z_device(r))
            )
            for r in range(1, t.grid.nz)
        }

    def finish(self):
        t = self.site
        self.local.wait()
        for r, slot in self.slots.items():
            t.copies.arrived(slot, self.got_z.at[r - 1])
        add_rows(
            self.out,
            [self.own] + [self.got_z.at[r - 1] for r in range(1, t.grid.nz)],
            0,
            self.rows,
        )


def load_in_turn(blocks):
    depth = blocks[0][0].mine.shape[0]
    for i, (flow, n) in enumerate(blocks):
        if n == 0:
            flow.base = i
    for i, (flow, n) in enumerate(blocks):
        if i < depth:
            flow.load(n)
        if i + depth < len(blocks):
            later, m = blocks[i + depth]
            flow.then[n] = functools.partial(later.load, m)


def scatter_scratch(grid, rows, cols, mine=True):
    block = (rows, cols)
    widest = max(grid.ax, grid.ay)
    depth = 3 if grid.nz <= 4 else 2
    found = [pltpu.VMEM((depth, grid.ay, grid.ax) + block, bf16)] if mine else []
    return found + [
        pltpu.VMEM((grid.nz, grid.ay, grid.ax) + block, bf16),
        pltpu.VMEM((grid.nz, max(1, widest - 1), widest) + block, bf16),
        pltpu.VMEM((grid.nz, max(1, widest - 1)) + block, bf16),
        pltpu.VMEM((max(1, grid.nz - 1),) + block, bf16),
    ]


def by_distance(size):
    return sorted(range(1, size), key=lambda r: (min(r, size - r), r))


class ExchangeFlow:
    def __init__(self, site, in_ref, out_ref, head=None, part=None):
        self.site, self.src, self.dst = site, in_ref, out_ref
        self.index = () if head is None else (head,) if part is None else (head, part)
        self.slots = {}

    def at(self, ref, n):
        return ref.at[(n,) + self.index]

    def start_one(self, r):
        t, ns = self.site, self.site.grid.ns
        if r == 0:
            self.own = t.local(lambda: (self.at(self.src, t.s), self.at(self.dst, t.s)))
            return
        self.slots[r] = t.copies.send(
            lambda: (
                self.at(self.src, turn(t.s, r, ns)),
                self.at(self.dst, t.s),
                (t.p, turn(t.s, r, ns)),
            )
        )

    def start(self):
        for r in by_distance(self.site.grid.ns)[::-1] + [0]:
            self.start_one(r)

    def finish(self):
        t, ns = self.site, self.site.grid.ns
        self.own.wait()
        for r, slot in self.slots.items():
            t.copies.arrived(slot, self.at(self.dst, turn(t.s, ns - r, ns)))


class SpreadFlow:
    def __init__(self, site, in_ref, out_ref, over_dp=False):
        self.site, self.src, self.dst, self.over_dp = site, in_ref, out_ref, over_dp
        g = site.grid
        self.size, self.place = (g.np, site.p) if over_dp else (g.ns, site.s)

    def start(self):
        t = self.site

        def refs(r):
            to = turn(self.place, r, self.size)
            return self.src, self.dst.at[self.place], (to, t.s) if self.over_dp else (t.p, to)

        self.slots = {
            r: t.copies.send(functools.partial(refs, r)) for r in by_distance(self.size)
        }
        self.own = t.local(lambda: (self.src, self.dst.at[self.place]))

    def finish(self):
        self.own.wait()
        for r, slot in self.slots.items():
            self.site.copies.arrived(slot, self.dst.at[turn(self.place, self.size - r, self.size)])


def flip(block):
    return jnp.transpose(block.astype(f32))


def attend_head(qkv, head, keys, values):
    sources, rows = qkv.shape[0], qkv.shape[-1]
    for s in range(sources):
        at = slice(s * rows, (s + 1) * rows)
        keys[:, at] = qkv[s, head, 1]
        values[at, :] = flip(qkv[s, head, 2]).astype(bf16)


def attend_block(scale, qkv, head, block, out, wide, logs, keys, values, scores):
    sources, rows = qkv.shape[0], qkv.shape[-1]
    query = flip(qkv[block, head, 0]).astype(bf16)
    factor = scale * math.log2(math.e)
    peak = None
    for s in range(sources):
        at = slice(s * rows, (s + 1) * rows)
        part = jnp.dot(query, keys[:, at], preferred_element_type=f32)
        scores[:, at] = part
        top = jnp.max(part, axis=-1, keepdims=True)
        peak = top if peak is None else jnp.maximum(peak, top)
    peak = peak * factor
    total = jnp.zeros((rows, 1), f32)
    mixed = jnp.zeros((rows, HEAD_DIM), f32)
    for s in range(sources):
        at = slice(s * rows, (s + 1) * rows)
        part = jnp.exp2(scores[:, at] * factor - peak)
        total = total + jnp.sum(part, axis=-1, keepdims=True)
        mixed = mixed + jnp.dot(part.astype(bf16), values[at, :], preferred_element_type=f32)
    mixed = jnp.transpose(mixed / total)
    wide[head, block] = mixed
    out[block, head] = mixed.astype(bf16)
    logs[head, block] = jnp.transpose(jnp.broadcast_to(peak + jnp.log2(total), (rows, 8)))


def attend_scratch(qkv):
    sources, _, _, dim, rows = qkv.shape
    length = sources * rows
    return [
        pltpu.VMEM((dim, length), bf16),
        pltpu.VMEM((length, dim), bf16),
        pltpu.VMEM((rows, length), f32),
    ]


def attend_back_head(qkv, head, keys, key_rows, values, grad_k, grad_v):
    sources, rows = qkv.shape[0], qkv.shape[-1]
    for s in range(sources):
        at = slice(s * rows, (s + 1) * rows)
        keys[:, at] = qkv[s, head, 1]
        key_rows[at, :] = flip(qkv[s, head, 1]).astype(bf16)
        values[:, at] = qkv[s, head, 2]
    grad_k[...] = jnp.zeros_like(grad_k)
    grad_v[...] = jnp.zeros_like(grad_v)


def attend_back_block(
    scale, qkv, grad_in, wide, logs, head, block, out, keys, key_rows, values, grad_k, grad_v
):
    sources, rows = qkv.shape[0], qkv.shape[-1]
    query_t = qkv[block, head, 0]
    grad_t = grad_in[block, head]
    query = flip(query_t).astype(bf16)
    grad = flip(grad_t).astype(bf16)
    factor = scale * math.log2(math.e)
    inner = jnp.sum(grad_t.astype(f32) * wide[head, block], axis=0, keepdims=True)
    inner = jnp.transpose(jnp.broadcast_to(inner, (8, rows)))[:, 0:1]
    log_rows = jnp.transpose(logs[head, block])[:, 0:1]
    grad_q = jnp.zeros((rows, HEAD_DIM), f32)
    for s in range(sources):
        at = slice(s * rows, (s + 1) * rows)
        part = jnp.dot(query, keys[:, at], preferred_element_type=f32)
        probs = jnp.exp2(part * factor - log_rows)
        grad_p = jnp.dot(grad, values[:, at], preferred_element_type=f32)
        grad_s = (probs * (grad_p - inner)).astype(bf16)
        grad_q = grad_q + jnp.dot(grad_s, key_rows[at, :], preferred_element_type=f32)
        grad_k[:, at] += jnp.dot(query_t, grad_s, preferred_element_type=f32)
        grad_v[:, at] += jnp.dot(grad_t, probs.astype(bf16), preferred_element_type=f32)
    out[block, head, 0] = jnp.transpose(grad_q * scale).astype(bf16)


def attend_back_end(scale, head, out, grad_k, grad_v):
    sources, rows = out.shape[0], out.shape[-1]
    for s in range(sources):
        at = slice(s * rows, (s + 1) * rows)
        out[s, head, 1] = (grad_k[:, at] * scale).astype(bf16)
        out[s, head, 2] = grad_v[:, at].astype(bf16)


def attend_back_scratch(qkv):
    sources, _, _, dim, rows = qkv.shape
    length = sources * rows
    return [
        pltpu.VMEM((dim, length), bf16),
        pltpu.VMEM((length, dim), bf16),
        pltpu.VMEM((dim, length), bf16),
        pltpu.VMEM((dim, length), f32),
        pltpu.VMEM((dim, length), f32),
    ]


VMEM = pl.BlockSpec(memory_space=pltpu.VMEM)
HBM = pl.BlockSpec(memory_space=pltpu.HBM)


def gather_shape(grid, rows, cols):
    return jax.ShapeDtypeStruct((grid.ay, grid.ax, grid.nz, grid.nc, rows, cols), bf16)


def gather_slots(grid):
    across = 2 * (grid.ax + grid.ay - 2) + 2 * (grid.ax - 1) * (grid.ay - 1)
    return grid.nz + 6 + grid.nz * (across + 1)


def scatter_slots(grid):
    return grid.nz * (2 * (grid.ax + grid.ay - 2) + 1) + grid.nz - 1


def move(grid, kernel, name, slots, locals_, call_id, out_shape, out_specs, in_specs, scratch, args, vmem, cost=None):
    return pl.pallas_call(
        functools.partial(kernel, grid),
        name=name,
        out_shape=out_shape,
        in_specs=in_specs,
        out_specs=out_specs,
        scratch_shapes=list(scratch)
        + [
            pltpu.SemaphoreType.DMA((slots,)),
            pltpu.SemaphoreType.DMA((slots,)),
            pltpu.SemaphoreType.DMA((locals_,)),
        ],
        compiler_params=pltpu.CompilerParams(
            collective_id=call_id, has_side_effects=True, vmem_limit_bytes=vmem * MIB
        ),
        cost_estimate=cost,
    )(*args)


def planned(steps, times, when):
    inside, rest = [], []
    at = 0
    for kind, n, step in steps:
        while at < len(times) and times[at] < when(kind, n):
            at += 1
        if at < len(times):
            inside.append((at, step))
        else:
            rest.append((kind, n, step))
    return inside, rest


def attention_kernel(
    grid,
    scale,
    own_0,
    own_a,
    own_b,
    own_c,
    table_ref,
    time_ref,
    lat,
    text,
    out_0,
    out_a,
    out_b,
    out_c,
    back_ref,
    qkv,
    wide,
    logs,
    a1,
    biases,
    z1,
    x2,
    c1,
    cq,
    ck,
    cv,
    oc,
    a2,
    *refs,
):
    mixed, keys, values, scores, table_all, parts, weights, att, sems = refs[:9]
    site = Site(grid, *refs[9:])
    heads, sources = qkv.shape[1], qkv.shape[0]
    tokens, width = a1.shape
    cols = weights.shape[4]
    cw = cols // 4
    rows = own_0.shape[0]
    nz, nc = grid.nz, grid.nc
    flows = [
        GatherFlow(site, out, own)
        for out, own in ((out_0, own_0), (out_a, own_a), (out_b, own_b), (out_c, own_c))
    ]
    incoming = [ExchangeFlow(site, parts, qkv, h) for h in range(heads)]
    outgoing = [ExchangeFlow(site, mixed, back_ref, h) for h in range(heads)]
    table = SpreadFlow(site, table_ref, table_all)
    table.start()
    flows[0].start()
    flows[0].zone.start()
    flows[0].first(0)
    for flow in flows[1:]:
        flow.start()
    relays = [flow.relays() for flow in flows]
    zones = [[("Z", k, flow.zone.start)] for k, flow in enumerate(flows)]
    steps = weave(
        sequence([block for flow in flows for block in flow.blocks()]),
        {
            ("F", 0): relays[0][:1],
            ("F", 1): relays[0][1:2],
            ("S", 0): relays[0][2:] + zones[1],
            ("S", 1): relays[1][:1],
            ("F", 3): relays[1][1:2],
            ("S", 2): relays[1][2:] + zones[2],
            ("S", 3): relays[2][:1],
            ("F", 5): relays[2][1:2],
            ("S", 4): relays[2][2:],
        },
    )[1:]

    normed, _ = norm_parts(lat[...].astype(f32))
    table.finish()
    part = table_ref.shape[1]
    for n in range(grid.ns):
        biases[:, n * part : (n + 1) * part] = table_all[n].astype(f32)
    shift = biases[0:1, :] + time_ref[0:1, :].astype(f32)
    gain = 1.0 + biases[1:2, :] + time_ref[1:2, :].astype(f32)
    a1[...] = (normed * gain + shift).astype(bf16)

    cut = max(i for i, (kind, n, _) in enumerate(steps) if kind == "T" and n == nz - 1) + 1
    run(steps[:cut])
    flows[0].finish()

    order = [(out, p) for out in (out_0, out_0, out_a, out_a) for p in range(grid.np)]

    def load(k):
        out, p = order[k]
        return pltpu.make_async_copy(
            out.at[p // grid.ax, p % grid.ax], weights.at[k % 2], sems.at[k % 2]
        )

    def through(left, k, lo, hi):
        slot = weights.at[k % 2]
        if rows % 16 == 0:
            return dot(left[...], slot[:, :, :, lo:hi].reshape(width, hi - lo))
        found = None
        for n in range(nz * nc):
            piece = dot(left[:, n * rows : (n + 1) * rows], slot[n // nc, n % nc, :, lo:hi])
            found = piece if found is None else found + piece
        return found

    def used(k):
        if k + 2 < len(order):
            load(k + 2).start()

    load(0).start()
    load(1).start()
    for p in range(grid.np):
        load(p).wait()
        found = through(a1, p, 0, 3 * cw)
        used(p)
        found = jnp.transpose(found)
        at = slice(p * cw, (p + 1) * cw)
        rows_q = jnp.transpose(jnp.broadcast_to(biases[6:7, at], (8, cw)))[:, 0:1]
        rows_v = jnp.transpose(jnp.broadcast_to(biases[7:8, at], (8, cw)))[:, 0:1]
        thirds = (found[0:cw] + rows_q, found[cw : 2 * cw], found[2 * cw : 3 * cw] + rows_v)
        for h in range(cw // HEAD_DIM):
            device, head = divmod(p * (cw // HEAD_DIM) + h, heads)
            for j in range(3):
                parts[device, head, j] = thirds[j][h * HEAD_DIM : (h + 1) * HEAD_DIM].astype(bf16)
    incoming[0].start()

    def due(kind, n):
        return 11.5 * n + {"F": -6, "S": 12, "T": 24, "P": 0, "Z": 0}[kind]

    cut_b = max([i + 1 for i, (kind, n, _) in enumerate(steps) if due(kind, n) <= 86] + [cut])
    run(steps[cut:cut_b])
    incoming[0].finish()
    for flow in incoming[1:2]:
        flow.start()
    times = [92 + 29 * (i // sources) + 2.4 * (i % sources) for i in range(heads * sources)]
    inside, rest = planned(steps[cut_b:], times, due)
    for n, (_, _, step) in enumerate(zones[3] + relays[3]):
        inside.append(((heads - 1) * sources + min(2 * n, sources - 1), step))

    def turn_of(i, carry):
        head, block = i // sources, turn(site.s, i, sources)
        for h in range(1, heads):

            @pl.when(i == h * sources)
            def _():
                incoming[h].finish()
                for flow in incoming[h + 1 : h + 2]:
                    flow.start()

        @pl.when(i % sources == 0)
        def _():
            attend_head(qkv, head, keys, values)

        attend_block(scale, qkv, head, block, mixed, wide, logs, keys, values, scores)
        for h in range(heads):
            for r in range(sources):
                pl.when(i == h * sources + r)(functools.partial(outgoing[h].start_one, r))
        for at in sorted({n for n, _ in inside}):

            @pl.when(i == at)
            def _():
                for n, step in inside:
                    if n == at:
                        step()

        return carry

    lax.fori_loop(0, heads * sources, turn_of, 0)

    def advance(count):
        run(rest[:count])
        del rest[:count]

    def vector(n):
        return biases[n : n + 1, :] + time_ref[n : n + 1, :].astype(f32)

    advance(max([i + 1 for i, (_, n, _) in enumerate(rest) if n < 2 * nz] + [0]))
    flows[1].finish()
    for flow in outgoing:
        flow.finish()
    for n in range(sources * heads):
        at = slice(n * HEAD_DIM, (n + 1) * HEAD_DIM)
        att[:, at] = flip(back_ref[n // heads, n % heads]).astype(bf16)
    k = grid.np
    for p in range(grid.np):
        at = slice(p * cw, (p + 1) * cw)
        load(k + p).wait()
        z1[:, at] = through(att, k + p, 3 * cw, 4 * cw) + biases[8:9, at]
        used(k + p)
    advance(2)
    x1 = lat[...].astype(f32) + vector(2) * z1[...]
    x2[...] = x1
    c1[...] = x1.astype(bf16)
    k += grid.np
    for p in range(grid.np):
        at = slice(p * cw, (p + 1) * cw)
        load(k + p).wait()
        ck[:, at] = through(text, k + p, cw, 2 * cw).astype(bf16)
        cv[:, at] = (through(text, k + p, 2 * cw, 3 * cw) + biases[10:11, at]).astype(bf16)
        cq[:, at] = (through(c1, k + p, 0, cw) + biases[9:10, at]).astype(bf16)
        used(k + p)
    advance(2)
    for h in range(width // HEAD_DIM):
        at = slice(h * HEAD_DIM, (h + 1) * HEAD_DIM)
        probs = cross_probs(scale, cq[:, at], ck[:, at])
        oc[:, at] = dot(probs.astype(bf16), cv[:, at]).astype(bf16)
        if h == width // HEAD_DIM // 2:
            advance(2)
    advance(2)
    k += grid.np
    for p in range(grid.np):
        at = slice(p * cw, (p + 1) * cw)
        load(k + p).wait()
        x2[:, at] = x2[:, at] + through(oc, k + p, 3 * cw, 4 * cw) + biases[11:12, at]
        used(k + p)
    normed, _ = norm_parts(x2[...])
    a2[...] = (normed * (1.0 + vector(4)) + vector(3)).astype(bf16)
    advance(len(rest))
    for flow in flows[2:]:
        flow.finish()
    site.copies.finish()


def attention(grid, scale, owns, table, time, lat, text):
    rows, cols = owns[0].shape
    tokens, width = lat.shape
    sources = grid.ns
    heads = width // HEAD_DIM // sources
    length = sources * tokens
    blocks = jax.ShapeDtypeStruct((sources, heads, 3, HEAD_DIM, tokens), bf16)
    low = jax.ShapeDtypeStruct((tokens, width), bf16)
    high = jax.ShapeDtypeStruct((tokens, width), f32)
    word = jax.ShapeDtypeStruct(text.shape, bf16)
    return move(
        grid,
        lambda g, *refs: attention_kernel(g, scale, *refs),
        "attention",
        4 * gather_slots(grid) + 2 * grid.ns * heads + grid.ns,
        5 + 2 * heads,
        1,
        [gather_shape(grid, rows, cols)] * 4
        + [
            jax.ShapeDtypeStruct((sources, heads, HEAD_DIM, tokens), bf16),
            blocks,
            jax.ShapeDtypeStruct((heads, sources, HEAD_DIM, tokens), f32),
            jax.ShapeDtypeStruct((heads, sources, 8, tokens), f32),
            jax.ShapeDtypeStruct((tokens, width), bf16),
            jax.ShapeDtypeStruct((table.shape[0], width), f32),
            high,
            high,
            low,
            low,
            word,
            word,
            low,
            low,
        ],
        [HBM] * 4 + [VMEM] * 14,
        [HBM] * 4 + [VMEM] * 4,
        [pltpu.VMEM((sources, heads, HEAD_DIM, tokens), bf16)]
        + attend_scratch(blocks)
        + [
            pltpu.VMEM((grid.ns,) + table.shape, bf16),
            pltpu.VMEM(blocks.shape, bf16),
            pltpu.VMEM((2, grid.nz, grid.nc, rows, cols), bf16),
            pltpu.VMEM((tokens, width), bf16),
            pltpu.SemaphoreType.DMA((2,)),
        ],
        owns + (table, time, lat, text),
        56,
        pl.CostEstimate(
            flops=4 * heads * length * length * HEAD_DIM,
            bytes_accessed=60 * MIB,
            transcendentals=heads * length * length,
        ),
    )


def attention_back_kernel(
    grid,
    scale,
    grad_a,
    grad_b,
    in_ref,
    text_ref,
    qkv,
    wide,
    logs,
    own_ref,
    column_ref,
    back_ref,
    words_ref,
    *refs,
):
    scratch_a, scratch_b = refs[:5], refs[5:9]
    refs = refs[9:]
    text_got, text_low, grad_in, grad_qkv, keys, key_rows, values, grad_k, grad_v = refs[:9]
    site = Site(grid, *refs[9:])
    heads, sources = qkv.shape[1], qkv.shape[0]
    incoming = [ExchangeFlow(site, in_ref, grad_in, h) for h in range(heads)]
    text = ExchangeFlow(site, text_ref, text_got)
    queries = [ExchangeFlow(site, grad_qkv, back_ref, h, 0) for h in range(heads)]
    outgoing = [ExchangeFlow(site, grad_qkv, back_ref, h, pl.ds(1, 2)) for h in range(heads)]
    mine = scratch_a[0]
    a = ScatterFlow(site, grad_a, own_ref.at[0], *scratch_a)
    b = ScatterFlow(site, grad_b, None, mine, *scratch_b, column_ref=column_ref)
    blocks = a.blocks() + b.blocks()
    incoming[0].start()
    load_in_turn(blocks)
    steps = sequence(blocks)

    def due(kind, n):
        return 11.5 * n + {"F": 4, "S": 18, "T": 30}[kind]

    cut = max(i for i, (kind, n, _) in enumerate(steps) if due(kind, n) <= 10) + 1
    run(steps[:cut])
    incoming[0].finish()
    for flow in incoming[1:]:
        flow.start()
    text.start()
    times = [14 + 4.6 * i for i in range(heads * sources)]
    inside, rest = planned(steps[cut:], times, due)
    words = SpreadFlow(site, text_low, words_ref)

    def sum_text():
        text.finish()
        total = text_got[0].astype(f32)
        for n in range(1, grid.ns):
            total = total + text_got[n].astype(f32)
        text_low[...] = total.astype(bf16)
        words.start()

    inside.append((sources - 1, sum_text))

    def turn_of(i, carry):
        head, block = i // sources, turn(site.s, i, sources)
        for h in range(1, heads):
            pl.when(i == h * sources)(incoming[h].finish)

        @pl.when(i % sources == 0)
        def _():
            attend_back_head(qkv, head, keys, key_rows, values, grad_k, grad_v)

        attend_back_block(
            scale, qkv, grad_in, wide, logs, head, block, grad_qkv, keys, key_rows, values, grad_k, grad_v
        )

        @pl.when(i % sources == sources - 1)
        def _():
            attend_back_end(scale, head, grad_qkv, grad_k, grad_v)

        for h in range(heads):
            for r in range(sources):
                pl.when(i == h * sources + r)(functools.partial(queries[h].start_one, r))
            pl.when(i == (h + 1) * sources - 1)(outgoing[h].start)
        for at in sorted({n for n, _ in inside}):

            @pl.when(i == at)
            def _():
                for n, step in inside:
                    if n == at:
                        step()

        return carry

    lax.fori_loop(0, heads * sources, turn_of, 0)
    run(rest)
    for flow in [a, b, words] + queries + outgoing:
        flow.finish()
    site.copies.finish()


def attention_back(grid, scale, grads, blocks, text, qkv, wide, logs, rows, cols):
    shape = (grid.ay, grid.ax, grid.nz, grid.nc, rows, cols)
    sources, heads, _, dim, tokens = qkv.shape
    length = sources * tokens
    return move(
        grid,
        lambda g, *refs: attention_back_kernel(g, scale, *refs),
        "attention_back",
        2 * scatter_slots(grid) + grid.ns * (2 + 3 * heads),
        2 * grid.nz + 2 + 3 * heads,
        2,
        [
            jax.ShapeDtypeStruct((1, rows, cols), f32),
            jax.ShapeDtypeStruct((grid.nz, rows, cols), bf16),
            jax.ShapeDtypeStruct(qkv.shape, bf16),
            jax.ShapeDtypeStruct(text.shape, bf16),
        ],
        [VMEM, VMEM, HBM, HBM],
        [HBM] * 4 + [VMEM] * 3,
        scatter_scratch(grid, rows, cols)
        + scatter_scratch(grid, rows, cols, mine=False)
        + [
            pltpu.VMEM(text.shape, bf16),
            pltpu.VMEM(text.shape[1:], bf16),
            pltpu.VMEM((sources, heads, dim, tokens), bf16),
            pltpu.VMEM(qkv.shape, bf16),
        ]
        + attend_back_scratch(qkv),
        tuple(g.reshape(shape) for g in grads) + (blocks, text, qkv, wide, logs),
        60,
        pl.CostEstimate(
            flops=10 * heads * length * length * dim,
            bytes_accessed=60 * MIB,
            transcendentals=heads * length * length,
        ),
    )


def dot(left, right, kind="nn"):
    contract = ((0 if kind[0] == "t" else 1,), (1 if kind[1] == "t" else 0,))
    return lax.dot_general(left, right, (contract, ((), ())), preferred_element_type=f32)


def norm_parts(tokens_in):
    center = tokens_in - jnp.mean(tokens_in, axis=-1, keepdims=True)
    spread = jnp.mean(center * center, axis=-1, keepdims=True)
    rate = lax.rsqrt(spread + norm_eps)
    return center * rate, rate


def norm_back(grad, normed, rate, gain):
    inner = grad * gain
    mean = jnp.mean(inner, axis=-1, keepdims=True)
    along = jnp.mean(inner * normed, axis=-1, keepdims=True)
    return rate * (inner - mean - normed * along)


def column(rows_ref, n):
    return rows_ref[n : n + 1, :]


def cross_probs(scale, query, keys):
    scores = dot(query, keys, "nt") * scale
    part = jnp.exp(scores - jnp.max(scores, axis=-1, keepdims=True))
    return part / jnp.sum(part, axis=-1, keepdims=True)


def gelu_pair(pre):
    rate = math.sqrt(2.0 / math.pi)
    square = pre * pre
    bend = jnp.tanh(rate * pre * (1.0 + 0.044715 * square))
    half = 0.5 * (1.0 + bend)
    slope = half + 0.5 * pre * (1.0 - bend * bend) * rate * (1.0 + 3 * 0.044715 * square)
    return pre * half, slope


def mlp_kernel(
    a2, cot, x2, up, down, b1, rows_ref, out, da2, grad_up, grad_down, du_sum, sums, a2_t, dz3, dz3_t, z3
):
    p = pl.program_id(0)

    @pl.when(p == 0)
    def _():
        back = (column(rows_ref, 0) * cot[...].astype(f32)).astype(bf16)
        dz3[...] = back
        dz3_t[...] = flip(back).astype(bf16)
        a2_t[...] = flip(a2[...]).astype(bf16)
        sums[0:1, :] = jnp.sum(back.astype(f32), axis=0, keepdims=True)

    pre = dot(a2[...], up[0]) + b1[0]
    act, slope = gelu_pair(pre)
    hidden = act.astype(bf16)
    grad = (dot(dz3[...], down[0]) * slope).astype(bf16)
    du_sum[0] = jnp.sum(grad.astype(f32), axis=0, keepdims=True)
    part = dot(hidden, down[0], "nt")
    back = dot(grad, up[0], "nt")

    @pl.when(p == 0)
    def _():
        z3[...] = part
        da2[...] = back

    @pl.when(p > 0)
    def _():
        z3[...] += part
        da2[...] += back

    grad_up[0] = dot(a2_t[...], grad).astype(bf16)
    grad_down[0] = dot(dz3_t[...], hidden).astype(bf16)

    @pl.when(p == pl.num_programs(0) - 1)
    def _():
        branch = z3[...] + column(rows_ref, 1)
        out[...] = (x2[...] + column(rows_ref, 0) * branch).astype(bf16)
        sums[1:2, :] = jnp.sum(cot[...].astype(f32) * branch, axis=0, keepdims=True)


def mlp(a2, cot, x2, up, down, b1, rows):
    tokens, width = a2.shape
    np_, _, cols = up.shape
    block = pl.BlockSpec((1, width, cols), lambda p: (p, 0, 0))
    row = pl.BlockSpec((1, 1, cols), lambda p: (p, 0, 0))
    return pl.pallas_call(
        mlp_kernel,
        name="mlp",
        grid=(np_,),
        out_shape=[
            jax.ShapeDtypeStruct((tokens, width), bf16),
            jax.ShapeDtypeStruct((tokens, width), f32),
            jax.ShapeDtypeStruct(up.shape, bf16),
            jax.ShapeDtypeStruct(down.shape, bf16),
            jax.ShapeDtypeStruct((np_, 1, cols), f32),
            jax.ShapeDtypeStruct((8, width), f32),
        ],
        in_specs=[VMEM, VMEM, VMEM, block, block, row, VMEM],
        out_specs=[VMEM, VMEM, block, block, row, VMEM],
        scratch_shapes=[
            pltpu.VMEM((width, tokens), bf16),
            pltpu.VMEM((tokens, width), bf16),
            pltpu.VMEM((width, tokens), bf16),
            pltpu.VMEM((tokens, width), f32),
        ],
        compiler_params=pltpu.CompilerParams(vmem_limit_bytes=56 * MIB),
        cost_estimate=pl.CostEstimate(
            flops=12 * tokens * width * cols * np_,
            bytes_accessed=44 * MIB,
            transcendentals=tokens * cols * np_,
        ),
    )(a2, cot, x2, up, down, b1, rows)


def cross_back_kernel(
    grid,
    scale,
    da2,
    x2,
    cot,
    z1,
    cq,
    ck,
    cv,
    c1,
    oc,
    text,
    rows_ref,
    w_self,
    w_cross,
    grad_ref,
    dx1,
    do_t,
    dz1,
    text_part,
    sums,
    own_ref,
    grad_cross,
    *refs,
):
    scratch, refs = refs[:5], refs[5:]
    doc, dz2, dcq, part_k, part_v, left, wo, wc, stage, sems = refs[:10]
    low = doc
    np_, width, wide = w_self.shape
    cw = wide // 4
    lo = 3 * cw // 128 * 128
    load_o = pltpu.make_async_copy(w_self.at[:, :, pl.ds(lo, wide - lo)], wo, sems.at[0])
    load_c = pltpu.make_async_copy(w_cross, wc, sems.at[1])
    load_c.start()
    load_o.start()
    site = Site(grid, *refs[10:])
    flow = ScatterFlow(site, grad_ref, own_ref.at[0], *scratch)
    load_in_turn(flow.blocks())
    steps = sequence(flow.blocks())

    def advance(count):
        run(steps[:count])
        del steps[:count]

    def total(n, matrix):
        sums[n : n + 1, :] = jnp.sum(matrix, axis=0, keepdims=True)

    normed, rate = norm_parts(x2[...])
    grad = da2[...]
    total(0, grad)
    total(1, grad * normed)
    grad = cot[...].astype(f32) + norm_back(grad, normed, rate, 1.0 + column(rows_ref, 0))
    dx1[...] = grad
    dz2[...] = grad.astype(bf16)
    total(2, dz2[...].astype(f32))
    advance(2)
    load_c.wait()

    def back(source, w, first):
        found = None
        for p in range(np_):
            part = dot(source[:, p * cw : (p + 1) * cw], w[p, :, first : first + cw], "nt")
            found = part if found is None else found + part
        return found

    doc[...] = back(dz2, wc, 3 * cw).astype(bf16)
    advance(1)
    half = width // HEAD_DIM // 2
    for h in range(width // HEAD_DIM):
        at = slice(h * HEAD_DIM, (h + 1) * HEAD_DIM)
        query, keys, grad_h = cq[:, at], ck[:, at], doc[:, at]
        probs = cross_probs(scale, query, keys)
        grad_p = dot(grad_h, cv[:, at], "nt")
        inner = jnp.sum(grad_p * probs, axis=-1, keepdims=True)
        grad_s = (probs * (grad_p - inner)).astype(bf16)
        dcq[:, at] = (dot(grad_s, keys) * scale).astype(bf16)
        part_k[:, at] = (dot(grad_s, query, "tn") * scale).astype(bf16)
        whole = dot(probs.astype(bf16), grad_h, "tn")
        part_v[:, at] = whole.astype(bf16)
        sums[4:5, at] = jnp.sum(whole, axis=0, keepdims=True)
        if h == half:
            advance(2)
    total(3, dcq[...].astype(f32))
    advance(2)
    grad = dx1[...] + back(dcq, wc, 0)
    dx1[...] = grad
    total(5, grad * z1[...])
    low[...] = (column(rows_ref, 1) * grad).astype(bf16)
    total(6, low[...].astype(f32))
    for p in range(np_):
        dz1[p] = low[:, p * cw : (p + 1) * cw]
    load_o.wait()
    do_t[...] = jnp.transpose(back(low, wo, 3 * cw - lo)).astype(bf16)
    advance(1)
    words = ck.shape[0]
    text_part[...] = jnp.zeros_like(text_part)
    text_part[0:words, 0:width] = part_k[...]
    text_part[0:words, width : 2 * width] = part_v[...]
    left[0] = flip(c1[...]).astype(bf16)
    left[1] = flip(oc[...]).astype(bf16)
    words_t = flip(text[...]).astype(bf16)

    def store(p):
        return pltpu.make_async_copy(stage.at[p % 2], grad_cross.at[p], sems.at[2 + p % 2])

    for p in range(np_):
        at = slice(p * cw, (p + 1) * cw)
        if p >= 2:
            store(p - 2).wait()
        into = stage.at[p % 2]
        into[:, 0:cw] = dot(left[0], dcq[:, at]).astype(bf16)
        into[:, cw : 2 * cw] = dot(words_t, part_k[:, at]).astype(bf16)
        into[:, 2 * cw : 3 * cw] = dot(words_t, part_v[:, at]).astype(bf16)
        into[:, 3 * cw : 4 * cw] = dot(left[1], dz2[:, at]).astype(bf16)
        store(p).start()
        if p % (np_ // 4 if np_ >= 4 else 1) == 0:
            advance(1)
    advance(len(steps))
    for p in range(max(0, np_ - 2), np_):
        store(p).wait()
    flow.finish()
    site.copies.finish()


def cross_backward(grid, scale, da2, x2, cot, z1, cq, ck, cv, c1, oc, text, rows, w_self, w_cross, grad, rows_padded, own_rows):
    tokens, width = x2.shape
    np_, _, wide = w_self.shape
    words = ck.shape[0]
    lo = 3 * (wide // 4) // 128 * 128
    low = pltpu.VMEM((tokens, width), bf16)
    word = pltpu.VMEM((words, width), bf16)
    return move(
        grid,
        lambda g, *refs: cross_back_kernel(g, scale, *refs),
        "cross_backward",
        scatter_slots(grid),
        grid.nz,
        5,
        [
            jax.ShapeDtypeStruct((tokens, width), f32),
            jax.ShapeDtypeStruct((width, tokens), bf16),
            jax.ShapeDtypeStruct((np_, tokens, wide // 4), bf16),
            jax.ShapeDtypeStruct((rows_padded, 2 * width), bf16),
            jax.ShapeDtypeStruct((8, width), f32),
            jax.ShapeDtypeStruct((1, own_rows, wide), f32),
            jax.ShapeDtypeStruct(w_cross.shape, bf16),
        ],
        [VMEM] * 6 + [HBM],
        [VMEM] * 11 + [HBM] * 3,
        scatter_scratch(grid, own_rows, wide)
        + [
            low,
            low,
            low,
            word,
            word,
            pltpu.VMEM((2, width, tokens), bf16),
            pltpu.VMEM((np_, width, wide - lo), bf16),
            pltpu.VMEM(w_cross.shape, bf16),
            pltpu.VMEM((2, width, wide), bf16),
            pltpu.SemaphoreType.DMA((4,)),
        ],
        (
            da2,
            x2,
            cot,
            z1,
            cq,
            ck,
            cv,
            c1,
            oc,
            text,
            rows,
            w_self,
            w_cross,
            grad.reshape(grid.ay, grid.ax, grid.nz, grid.nc, own_rows, wide),
        ),
        63,
        pl.CostEstimate(
            flops=11 * tokens * width * width, bytes_accessed=50 * MIB, transcendentals=0
        ),
    )


def last_kernel(
    grid,
    a1,
    grad_qkv,
    att_t,
    dz1,
    lat,
    dx1,
    words,
    rows_ref,
    sums,
    mlp_sums,
    du_sums,
    own_up,
    own_down,
    w_self,
    w_cross,
    column_ref,
    own_ref,
    tokens_ref,
    words_ref,
    time_ref,
    own_table,
    norm_ref,
    *refs,
):
    scratch, refs = refs[:4], refs[4:]
    slab, a1_t, by_dp, back_t, weights, table_all, table_in = refs[:7]
    column_own, column_got = refs[7:9]
    table_got, table_sum, table_dp, tile, tile_got, tile_sum, tile_dp, sems = refs[9:17]
    np_, width, wide = w_self.shape
    tokens = a1.shape[0]
    cw = wide // 4
    nc, rows = grid.nc, wide and slab.shape[4]
    lo, hi = cw // 128 * 128, min(wide, -(-3 * cw // 128) * 128)
    loads = [
        pltpu.make_async_copy(w_self.at[p], weights.at[p % 2], sems.at[p % 2]) for p in range(np_)
    ] + [
        pltpu.make_async_copy(
            w_cross.at[p, :, pl.ds(lo, hi - lo)],
            weights.at[(np_ + p) % 2, :, pl.ds(0, hi - lo)],
            sems.at[(np_ + p) % 2],
        )
        for p in range(np_)
    ]
    loads[0].start()
    loads[1].start()

    def weight(k):
        loads[k].wait()
        return weights.at[k % 2]

    def used(k):
        if k + 2 < len(loads):
            loads[k + 2].start()

    site = Site(grid, *refs[17:])
    flow = NearScatterFlow(site, slab, own_ref.at[0], None, *scratch)
    column_sum = ColumnSum(site, column_ref, own_ref.at[1], column_own, column_got)
    column_sum.start()
    flat = flip(a1[...]).astype(bf16)
    span = nc * rows
    for z in range(grid.nz):
        a1_t[z] = flat[z * span : (z + 1) * span]
    heads = grad_qkv.shape[1]
    per_block = cw // HEAD_DIM
    for p in range(np_):
        for h in range(per_block):
            source, head = divmod(p * per_block + h, heads)
            for j in range(3):
                at = j * cw + h * HEAD_DIM
                by_dp[p, at : at + HEAD_DIM] = grad_qkv[source, head, j]

    for n in range(grid.nz):
        zone = flow.zone(n)
        for p in range(np_):
            part = dot(a1_t[zone], by_dp[p], "nt").astype(bf16)
            rest = dot(att_t[zone], dz1[p]).astype(bf16)
            for c in range(nc):
                at = slice(c * rows, (c + 1) * rows)
                slab[n, c, p // grid.ax, p % grid.ax, :, 0 : 3 * cw] = part[at]
                slab[n, c, p // grid.ax, p % grid.ax, :, 3 * cw :] = rest[at]
        flow.load(n)
        if n == 1:
            flow.first(0)
    steps = sequence(flow.blocks())[1:]

    def advance(count):
        run(steps[:count])
        del steps[:count]

    advance(2)
    for p in range(np_):
        part = dot(weight(p)[:, 0 : 3 * cw], by_dp[p])
        back_t[...] = part if p == 0 else back_t[...] + part
        used(p)
        if np_ < 8 or p % 4 == 0:
            advance(1)
    grad = jnp.transpose(back_t[...])
    normed, rate = norm_parts(lat[...].astype(f32))
    tokens_ref[...] = dx1[...] + norm_back(grad, normed, rate, 1.0 + column(rows_ref, 0))
    for at, source, n in (
        (2, sums, 5),
        (3, sums, 0),
        (4, sums, 1),
        (5, mlp_sums, 1),
        (8, sums, 6),
        (9, sums, 3),
        (10, sums, 4),
        (11, sums, 2),
        (12, mlp_sums, 0),
    ):
        table_all[at : at + 1, :] = source[n : n + 1, :]
    for p in range(np_):
        at, lane = 13 + p * wide // width, p * wide % width
        table_all[at : at + 1, lane : lane + wide] = du_sums[p]
    table_all[0:1, :] = jnp.sum(grad, axis=0, keepdims=True)
    table_all[1:2, :] = jnp.sum(grad * normed, axis=0, keepdims=True)
    ones = jnp.ones((8, tokens), bf16)
    for p in range(np_):
        whole = dot(ones, by_dp[p], "nt")
        at = slice(p * cw, (p + 1) * cw)
        table_all[6:7, at] = whole[0:1, 0:cw]
        table_all[7:8, at] = whole[0:1, 2 * cw : 3 * cw]
    part = width // grid.ns
    for n in range(grid.ns):
        table_in[n] = table_all[0 : table_in.shape[1], n * part : (n + 1) * part]
    table = ExchangeFlow(site, table_in, table_got)
    table.start()
    advance(2)
    found = None
    for p in range(np_):
        w = weight(np_ + p)
        at = slice(p * cw, (p + 1) * cw)
        both = dot(words[:, at], w[:, cw - lo : 2 * cw - lo], "nt")
        at = slice(width + p * cw, width + (p + 1) * cw)
        both = both + dot(words[:, at], w[:, 2 * cw - lo : 3 * cw - lo], "nt")
        found = both if found is None else found + both
        used(np_ + p)
    words_ref[...] = found[0 : words_ref.shape[0]]
    table.finish()
    total = table_got[0]
    for n in range(1, grid.ns):
        total = total + table_got[n]
    table_sum[...] = total
    whole = SpreadFlow(site, table_sum, time_ref)
    whole.start()
    over = SpreadFlow(site, table_sum, table_dp, over_dp=True)
    over.start()
    advance(max(0, len(steps) - 2))
    over.finish()
    total = table_dp[0]
    for n in range(1, grid.np):
        total = total + table_dp[n]
    own_table[...] = total
    column_sum.finish()
    square = jnp.sum(own_ref[1] * own_ref[1], keepdims=True)
    for done in (own_up, own_down):
        square = square + jnp.sum(done[0] * done[0], keepdims=True)
    square = square + jnp.where(site.p == 0, 1.0, 0.0) * jnp.sum(total * total, keepdims=True)
    advance(2)
    flow.finish()
    square = square + jnp.sum(own_ref[0] * own_ref[0], keepdims=True)
    tile[...] = jnp.broadcast_to(square, tile.shape)
    near = SpreadFlow(site, tile, tile_got)
    near.start()
    near.finish()
    total = tile_got[0]
    for n in range(1, grid.ns):
        total = total + tile_got[n]
    tile_sum[...] = total
    far = SpreadFlow(site, tile_sum, tile_dp, over_dp=True)
    far.start()
    far.finish()
    total = tile_dp[0]
    for n in range(1, grid.np):
        total = total + tile_dp[n]
    norm_ref[...] = total
    whole.finish()
    site.copies.finish()


def last_sums(grid, a1, grad_qkv, att_t, dz1, lat, dx1, words, text_count, rows_in, sums, owns, w_self, w_cross, column, table_rows):
    np_, width, wide = w_self.shape
    rows, cols = column.shape[1:]
    tokens = a1.shape[0]
    small = (table_rows, width // grid.ns)
    tile = (8, 128)
    return move(
        grid,
        last_kernel,
        "last_sums",
        scatter_slots(grid) + grid.nz + 3 * grid.ns + 2 * grid.np,
        6,
        3,
        [
            jax.ShapeDtypeStruct((2, rows, cols), f32),
            jax.ShapeDtypeStruct((tokens, width), f32),
            jax.ShapeDtypeStruct((text_count, width), f32),
            jax.ShapeDtypeStruct((grid.ns,) + small, f32),
            jax.ShapeDtypeStruct(small, f32),
            jax.ShapeDtypeStruct(tile, f32),
        ],
        [VMEM, VMEM, VMEM, HBM, VMEM, VMEM],
        [VMEM] * 13 + [HBM] * 3,
        scatter_scratch(grid, rows, cols, mine=False)
        + [
            pltpu.VMEM((grid.nz, grid.nc, grid.ay, grid.ax, rows, cols), bf16),
            pltpu.VMEM((grid.nz, grid.nc * rows, tokens), bf16),
            pltpu.VMEM((np_, 3 * (wide // 4), tokens), bf16),
            pltpu.VMEM((width, tokens), f32),
            pltpu.VMEM((2, width, wide), bf16),
            pltpu.VMEM((-(-table_rows // 8) * 8, width), f32),
            pltpu.VMEM((grid.ns,) + small, f32),
            pltpu.VMEM((rows, cols), bf16),
            pltpu.VMEM((max(1, grid.nz - 1), rows, cols), bf16),
            pltpu.VMEM((grid.ns,) + small, f32),
            pltpu.VMEM(small, f32),
            pltpu.VMEM((grid.np,) + small, f32),
            pltpu.VMEM(tile, f32),
            pltpu.VMEM((grid.ns,) + tile, f32),
            pltpu.VMEM(tile, f32),
            pltpu.VMEM((grid.np,) + tile, f32),
            pltpu.SemaphoreType.DMA((2,)),
        ],
        (
            a1,
            grad_qkv,
            att_t.reshape(grid.nz, grid.nc * rows, tokens),
            dz1,
            lat,
            dx1,
            words,
            rows_in,
            *sums,
            *owns,
            w_self,
            w_cross,
            column,
        ),
        60,
    )


def layer_norm(tokens_in):
    center = tokens_in - jnp.mean(tokens_in, axis=-1, keepdims=True)
    spread = jnp.mean(center * center, axis=-1, keepdims=True)
    return center * lax.rsqrt(spread + norm_eps)


def modulate(tokens_in, shift_row, scale_row):
    return layer_norm(tokens_in) * (1.0 + scale_row) + shift_row


def adam_step(weight, gradient, first_moment, second_moment, factor):
    clipped = gradient * factor
    first_new = first_decay * first_moment + (1.0 - first_decay) * clipped
    second_new = second_decay * second_moment + (1.0 - second_decay) * clipped * clipped
    first_hat = first_new / (1.0 - first_decay**STEP)
    second_hat = second_new / (1.0 - second_decay**STEP)
    updated = weight - learn_rate * (
        first_hat / (jnp.sqrt(second_hat) + adam_eps) + weight_decay * weight
    )
    return (updated, first_new, second_new)


def body(
    grid,
    latents,
    time_embed,
    text_tokens,
    cotangent,
    w_attn,
    w_mlp,
    bias_table,
    attn_first,
    attn_second,
    mlp_first,
    mlp_second,
    table_first,
    table_second,
):
    np_, ns = grid.np, grid.ns
    tokens_in = latents[0].astype(f32)
    rows, width = tokens_in.shape
    text_rows = text_tokens[0]
    text_count = text_rows.shape[0]
    heads = width // HEAD_DIM
    per_block = heads // np_
    local_heads = heads // ns
    scale = HEAD_DIM ** (-0.5)
    own_rows, own_cols = w_attn.shape[1], w_attn.shape[2]
    wide = 4 * own_cols

    def pack(matrices):
        return matrices.reshape(2, 4, own_rows, own_cols).transpose(0, 2, 1, 3).reshape(2, own_rows, wide)

    def unpack(slab):
        return slab.reshape(2, own_rows, 4, own_cols).transpose(0, 2, 1, 3).reshape(8, own_rows, own_cols)

    attn_low = pack(w_attn.astype(bf16))
    mlp_low = w_mlp.astype(bf16)
    own = (attn_low[0], attn_low[1], mlp_low[0], mlp_low[1])
    forward = attention(
        grid, scale, own, bias_table.astype(bf16), time_embed[0], latents[0], text_rows
    )
    w_self, w_cross, w_up, w_down = [w.reshape(np_, width, wide) for w in forward[:4]]
    attended_t, qkv, mixed_wide, logs, act_in, biases = forward[4:10]
    z1, x2, c1, cq, text_k, text_v, cross_out, a2 = forward[10:]
    modulation = biases[0:6] + time_embed[0].astype(f32)
    attended_t = attended_t.reshape(width, rows)

    block_out, da2, grad_up, grad_down, du_sums, mlp_sums = mlp(
        a2,
        cotangent[0],
        x2,
        w_up,
        w_down,
        biases[13:17].reshape(np_, 1, wide),
        jnp.stack([modulation[5], biases[12]]),
    )
    text_share = -(-text_count // (8 * ns)) * 8
    grad_first, grad_attended, dz1, text_part, sums, own_up, grad_cross = cross_backward(
        grid,
        scale,
        da2,
        x2,
        cotangent[0],
        z1,
        cq,
        text_k,
        text_v,
        c1,
        cross_out,
        text_rows,
        jnp.stack([modulation[4], modulation[2]]),
        w_self,
        w_cross,
        grad_up,
        ns * text_share,
        own_rows,
    )
    own_down, grad_column, grad_qkv, text_sum = attention_back(
        grid,
        scale,
        (grad_down, grad_cross),
        grad_attended.reshape(ns, local_heads, HEAD_DIM, rows),
        text_part.reshape(ns, text_share, 2 * width),
        qkv,
        mixed_wide,
        logs,
        own_rows,
        wide,
    )
    table_rows = bias_table.shape[0]
    own_mlp = jnp.concatenate([own_up, own_down], axis=0)
    own_attn, grad_tokens, grad_words, time_table, own_table, squares = last_sums(
        grid,
        act_in,
        grad_qkv,
        attended_t,
        dz1,
        latents[0],
        grad_first,
        text_sum.reshape(ns * text_share, 2 * width),
        text_count,
        modulation[1:2],
        (sums, mlp_sums, du_sums),
        (own_up, own_down),
        w_self,
        w_cross,
        grad_column,
        table_rows,
    )
    grad_time = time_table[:, :6].transpose(1, 0, 2).reshape(6, width)
    own_attn = unpack(own_attn)
    square_total = squares[0, 0]
    grad_norm = jnp.sqrt(square_total)
    factor = jnp.minimum(1.0, clip_norm / (grad_norm + 1e-06))
    attn_new, attn_first_new, attn_second_new = adam_step(
        w_attn, own_attn, attn_first, attn_second, factor
    )
    mlp_new, mlp_first_new, mlp_second_new = adam_step(
        w_mlp, own_mlp, mlp_first, mlp_second, factor
    )
    table_new, table_first_new, table_second_new = adam_step(
        bias_table, own_table, table_first, table_second, factor
    )
    return (
        block_out[None],
        grad_tokens[None],
        grad_time[None],
        grad_words[None],
        grad_norm,
        attn_new,
        attn_new.astype(bf16),
        attn_first_new,
        attn_second_new,
        mlp_new,
        mlp_new.astype(bf16),
        mlp_first_new,
        mlp_second_new,
        table_new,
        table_new.astype(bf16),
        table_first_new,
        table_second_new,
        own_table[12],
    )


def solution(mesh):
    return jax.shard_map(
        functools.partial(body, Grid(mesh)),
        mesh=mesh,
        in_specs=(
            P("dp", "seq", None),
            P("dp", None, None),
            P("dp", None, None),
            P("dp", "seq", None),
            P(None, "seq", "dp"),
            P(None, "seq", "dp"),
            P(None, "seq"),
            P(None, "seq", "dp"),
            P(None, "seq", "dp"),
            P(None, "seq", "dp"),
            P(None, "seq", "dp"),
            P(None, "seq"),
            P(None, "seq"),
        ),
        out_specs=(
            P("dp", "seq", None),
            P("dp", "seq", None),
            P("dp", None, None),
            P("dp", None, None),
            P(),
            P(None, "seq", "dp"),
            P(None, "seq", "dp"),
            P(None, "seq", "dp"),
            P(None, "seq", "dp"),
            P(None, "seq", "dp"),
            P(None, "seq", "dp"),
            P(None, "seq", "dp"),
            P(None, "seq", "dp"),
            P(None, "seq"),
            P(None, "seq"),
            P(None, "seq"),
            P(None, "seq"),
            P("seq"),
        ),
        check_vma=False,
    )
```

time: 1930 us -> 637 us (0.33)
  waiting for transfers between devices: 1030 us -> 0 us
  Pallas kernels: 0 us -> 597 us
  matrix products: 311 us -> 0 us
  local copies, waits for them, and re-layouts: 290 us -> 17.7 us
  blocking collectives: 142 us -> 0 us
  other arithmetic: 106 us -> 12.5 us
    pallas_call x0 -> x5, Pallas kernels: none -> 597 us  [the longest x4 553 us: move(): pl.pallas_call(functools.partial(kernel, grid), name=name, out_shape=out_...]
    reduce_scatter x3 -> x0, waiting for transfers between devices: 404 us -> none  [the longest x1 404 us: over_seq(): lax.psum_scatter(partials[0], 'seq', scatter_dimension=1, tiled=True)]
    all_to_all x4 -> x0, waiting for transfers between devices: 331 us -> none  [the longest x1 175 us: body(): lax.all_to_all(qkv_rows, 'seq', split_axis=2, concat_axis=0, tiled=True)]
    dot_general x71 -> x0, matrix products: 308 us -> none  [the longest x6 45.3 us: backward_block(): jnp.einsum('qhc,khc->hqk', grad_block, value_heads, preferred_element_typ...]
    all_gather x4 -> x0, waiting for transfers between devices: 268 us -> none  [the longest x1 173 us: body(): lax.all_gather(wide_parts[0], 'seq', axis=1, tiled=True)]
    unnamed x220 -> x32, local copies, waits for them, and re-layouts: 174 us -> 5.11 us
    psum x3 -> x0, blocking collectives: 128 us -> none  [the longest x1 71.8 us: body(): lax.psum((mod_part, part_k, part_v), 'seq')]
    convert_element_type x12 -> x3, other arithmetic: 47.3 us -> 2.96 us  [the longest x1 1.47 us: body(): bias_table.astype(bf16)]
  transfers between devices with their start and end apart: 13 -> 0, of which waited for: 9 -> 0; matrix products, arithmetic and copies ran while one was open for 30% -> 0% of each run, Pallas kernels for 0% -> 0%
where the time goes in v1:
time: 637 us; the launch traced here: 630 us
  Pallas kernels  597 us (94%)
  local copies, waits for them, and re-layouts  17.7 us (3%)
  other arithmetic  12.5 us (2%)
    pallas_call x4, Pallas kernels, move(): pl.pallas_call(functools.partial(kernel, grid), name=name, out_shape=out_...  553 us
    pallas_call x1, Pallas kernels, mlp(): pl.pallas_call(mlp_kernel, name='mlp', grid=(np_,), out_shape=[jax.ShapeD...  43.5 us

profile of v1, /device:TPU:0, one launch (start us, length us, event | category | flops | bytes accessed | tf_op | source)
XLA Modules:
  0.0 629.6 jit_solution(3145946932957823975)
XLA Ops:
  0.7 1.5 convert_element_type.23.refs_4_
  2.1 1.4 convert_element_type.22
  3.5 0.9 slice_bitcast_fusion
  5.2 1.0 squeeze.32.refs_1_
  6.2 1.0 squeeze.31.refs_0_
  7.3 246.0 %attention.1 = (bf16[2,2,4,2,144,1152]{5,4,3,2,1,0:T(8,128)(2,1)}, bf16[2,2,4,2,144,1152]{5,4,3,2,1,0:T(8,128)(2,1)}, bf16[2,2,4,2,144,1152]{5,4,3,2,1,0:T(8,128...) custom-call(bf16[144,1152]{1,0:T(8,128)(2,1)} %squeeze.31.refs_0_, ...), custom_call_target="tpu_custom_call" | custom-call | flops 5435817984 | bytes 62914560 | tf_op jit(solution)/shard_map/attention/pallas_call | solution.py:765
  253.3 0.8 slice.63
  254.0 0.9 slice.60
  254.9 0.8 convert_add_fusion
  257.5 43.5 %mlp.1 = (bf16[384,1152]{1,0:T(8,128)(2,1)}, f32[384,1152]{1,0:T(8,128)}, bf16[4,1152,1152]{2,1,0:T(8,128)(2,1)}, bf16[4,1152,1152]{2,1,0:T(8,128)(2,1)}, f32[4,1,1152]{2,1,0:T(1,128)}, /*index=5*/f32[8,1152]{1,0:T(8,128)}) custom-call(bf16[384,1152]{1,0:T(8,128)(2,1)} %get-tuple-element.59.a2, bf16[384,1152]{1,0:T(8,128)(2,1)} %bitcast.41, ...), custom_call_target="tpu_custom_call" | custom-call | flops 24461180928 | bytes 46137344 | tf_op jit(solution)/shard_map/mlp/pallas_call | solution.py:1286
  301.1 71.5 %cross_backward.1 = (f32[384,1152]{1,0:T(8,128)}, bf16[1152,384]{1,0:T(8,128)(2,1)}, bf16[4,384,288]{2,1,0:T(8,128)(2,1)}, bf16[128,2304]{1,0:T(8,128)(2,1)}, f3...) custom-call(f32[384,1152]{1,0:T(8,128)} %get-tuple-element.67.refs_0_, ...), custom_call_target="tpu_custom_call" | custom-call | flops 5605687296 | bytes 52428800 | tf_op jit(solution)/shard_map/cross_backward/pallas_call | solution.py:765
  372.6 138.4 %attention_back.1 = (f32[1,144,1152]{2,1,0:T(8,128)}, bf16[4,144,1152]{2,1,0:T(8,128)(2,1)}, bf16[8,2,3,72,384]{4,3,2,1,0:T(8,128)(2,1)}, bf16[8,16,2304]{2,1,0:T(8,128)(2,1)}) custom-call(bf16[2,2,4,2,144,1152]{5,4,3,2,1,0:T(8,128)(2,1)} %bitcast.57, bf16[2,2,4,2,144,1152]{5,4,3,2,1,0:T(8,128)(2,1)} %bitcast.52, bf16[8,2,72,384]{3,2,1,0:T(8,128)(2,1)} %bitcast.53, ...), custom_call_target="tpu_custom_call" | custom-call | flops 13589544960 | bytes 62914560 | tf_op jit(solution)/shard_map/attention_back/pallas_call | solution.py:765
  511.0 97.1 %last_sums.1 = (f32[2,144,1152]{2,1,0:T(8,128)}, f32[384,1152]{1,0:T(8,128)}, f32[120,1152]{1,0:T(8,128)}, f32[8,17,144]{2,1,0:T(8,128)}, f32[17,144]{1,0:T(8,128)}, /*index=5*/f32[8,128]{1,0:T(8,128)}) custom-call(bf16[384,1152]{1,0:T(8,128)(2,1)} %get-tuple-element.65.a1, bf16[8,2,3,72,384]{4,3,2,1,0:T(8,128)(2,1)} %get-tuple-element.83.grad_qkv, ...), custom_call_target="tpu_custom_call" | custom-call | tf_op jit(solution)/shard_map/last_sums/pallas_call | solution.py:765
  608.2 1.2 slice.68
  610.1 1.3 slice.73
  611.4 1.4 fusion.3
  612.7 0.8 slice_bitcast_fusion.2
  614.3 2.1 fusion.9
  616.7 1.1 copy-done.2
  618.2 3.0 fusion.5
  621.4 1.0 copy-done.6
  622.4 3.7 fusion.7
  626.1 1.2 copy.39
  627.5 0.8 copy.40
  (37 shorter events, 4.4 us)
Async XLA Ops:
  0.7 3.8 copy-start
  7.3 247.7 %copy-start.14 = (bf16[1,6,1152]{2,1,0:T(8,128)(2,1)S(1)}, bf16[1,6,1152]{2,1,0:T(8,128)(2,1)}, u32[]{:S(2)}) copy-start(bf16[1,6,1152]{2,1,0:T(8,128)(2,1)} %param.14) | copy-start | bytes 41476
  511.0 100.3 %copy-start.11 = (f32[17,144]{1,0:T(8,128)S(1)}, f32[17,144]{1,0:T(8,128)}, u32[]{:S(2)}) copy-start(f32[17,144]{1,0:T(8,128)} %param.19) | copy-start | bytes 29380
  511.0 100.3 %copy-start.12 = (f32[17,144]{1,0:T(8,128)S(1)}, f32[17,144]{1,0:T(8,128)}, u32[]{:S(2)}) copy-start(f32[17,144]{1,0:T(8,128)} %param.24) | copy-start | bytes 29380
  511.0 100.3 %copy-start.13 = (f32[17,144]{1,0:T(8,128)S(1)}, f32[17,144]{1,0:T(8,128)}, u32[]{:S(2)}) copy-start(f32[17,144]{1,0:T(8,128)} %param.25) | copy-start | bytes 29380
  614.3 2.2 copy-start.8
  614.3 2.4 copy-start.9
  616.4 1.4 copy-start.2
  616.4 1.5 copy-start.3
  616.4 1.7 copy-start.4
  618.2 3.0 copy-start.1
  618.2 3.2 copy-start.5
  618.2 4.2 copy-start.6
  622.4 3.7 copy-start.7
  626.1 1.4 copy-start.10

commit v2 on v1

--- a/solution.py
+++ b/solution.py
@@ -170,7 +170,7 @@
     return [(0, rows, i % 2 == 0)]
 
 
-def sequence(blocks, lead=2):
+def sequence(blocks, lead=1):
     steps = []
     for i in range(len(blocks) + 2):
         for ahead in range(lead + 1) if i == 0 else (lead,):
@@ -570,7 +570,7 @@
 def scatter_scratch(grid, rows, cols, mine=True):
     block = (rows, cols)
     widest = max(grid.ax, grid.ay)
-    depth = 3 if grid.nz <= 4 else 2
+    depth = min(grid.nz, 2)
     found = [pltpu.VMEM((depth, grid.ay, grid.ax) + block, bf16)] if mine else []
     return found + [
         pltpu.VMEM((grid.nz, grid.ay, grid.ax) + block, bf16),
@@ -916,7 +916,7 @@
     incoming[0].start()
 
     def due(kind, n):
-        return 11.5 * n + {"F": -6, "S": 12, "T": 24, "P": 0, "Z": 0}[kind]
+        return 11.5 * n + {"F": -16, "S": 2, "T": 14, "P": 0, "Z": 0}[kind]
 
     cut_b = max([i + 1 for i, (kind, n, _) in enumerate(steps) if due(kind, n) <= 86] + [cut])
     run(steps[cut:cut_b])
@@ -995,8 +995,8 @@
         at = slice(h * HEAD_DIM, (h + 1) * HEAD_DIM)
         probs = cross_probs(scale, cq[:, at], ck[:, at])
         oc[:, at] = dot(probs.astype(bf16), cv[:, at]).astype(bf16)
-        if h == width // HEAD_DIM // 2:
-            advance(2)
+        if h % max(1, width // HEAD_DIM // 4) == 0:
+            advance(1)
     advance(2)
     k += grid.np
     for p in range(grid.np):
@@ -1101,7 +1101,7 @@
     steps = sequence(blocks)
 
     def due(kind, n):
-        return 11.5 * n + {"F": 4, "S": 18, "T": 30}[kind]
+        return 11.5 * n + {"F": 4, "S": 14, "T": 22}[kind]
 
     cut = max(i for i, (kind, n, _) in enumerate(steps) if due(kind, n) <= 10) + 1
     run(steps[:cut])
@@ -1742,6 +1742,46 @@
     )
 
 
+def adam_kernel(
+    norm, grad_attn, grad_up, grad_down, w_attn, f_attn, s_attn, w_mlp, f_mlp, s_mlp, *outs
+):
+    factor = jnp.minimum(1.0, clip_norm / (norm[0:1, 0:1] + 1e-06))
+    width = w_attn.shape[2]
+    for j in range(w_attn.shape[0]):
+        grad = grad_attn[0, :, j * width : (j + 1) * width]
+        new, first, second = adam_step(w_attn[j], grad, f_attn[j], s_attn[j], factor)
+        outs[0][j], outs[1][j], outs[2][j], outs[3][j] = new, new.astype(bf16), first, second
+    grad = jnp.where(pl.program_id(0) == 0, grad_up[0], grad_down[0])
+    new, first, second = adam_step(w_mlp[0], grad, f_mlp[0], s_mlp[0], factor)
+    outs[4][0], outs[5][0], outs[6][0], outs[7][0] = new, new.astype(bf16), first, second
+
+
+def adam(norm, grad_attn, grad_up, grad_down, attn, mlp_state):
+    rows, cols = grad_up.shape[1:]
+    width = attn[0].shape[2]
+    part = rows // 3 if rows % 48 == 0 else rows
+    slab = pl.BlockSpec((1, part, cols), lambda k, r: (k, r, 0))
+    one = pl.BlockSpec((1, part, cols), lambda k, r: (0, r, 0))
+    four = pl.BlockSpec((4, part, width), lambda k, r: (k, r, 0))
+
+    def shapes(array):
+        full = jax.ShapeDtypeStruct(array.shape, f32)
+        return [full, jax.ShapeDtypeStruct(array.shape, bf16), full, full]
+
+    return pl.pallas_call(
+        adam_kernel,
+        name="adam",
+        grid=(2, rows // part),
+        out_shape=shapes(attn[0]) + shapes(mlp_state[0]),
+        in_specs=[VMEM, slab, one, one] + [four] * 3 + [slab] * 3,
+        out_specs=[four] * 4 + [slab] * 4,
+        compiler_params=pltpu.CompilerParams(vmem_limit_bytes=40 * MIB),
+        cost_estimate=pl.CostEstimate(
+            flops=40 * attn[0].size, bytes_accessed=24 * MIB, transcendentals=2 * attn[0].size
+        ),
+    )(norm, grad_attn, grad_up, grad_down, *attn, *mlp_state)
+
+
 def layer_norm(tokens_in):
     center = tokens_in - jnp.mean(tokens_in, axis=-1, keepdims=True)
     spread = jnp.mean(center * center, axis=-1, keepdims=True)
@@ -1794,9 +1834,6 @@
 
     def pack(matrices):
         return matrices.reshape(2, 4, own_rows, own_cols).transpose(0, 2, 1, 3).reshape(2, own_rows, wide)
-
-    def unpack(slab):
-        return slab.reshape(2, own_rows, 4, own_cols).transpose(0, 2, 1, 3).reshape(8, own_rows, own_cols)
 
     attn_low = pack(w_attn.astype(bf16))
     mlp_low = w_mlp.astype(bf16)
@@ -1853,7 +1890,6 @@
         wide,
     )
     table_rows = bias_table.shape[0]
-    own_mlp = jnp.concatenate([own_up, own_down], axis=0)
     own_attn, grad_tokens, grad_words, time_table, own_table, squares = last_sums(
         grid,
         act_in,
@@ -1873,15 +1909,25 @@
         table_rows,
     )
     grad_time = time_table[:, :6].transpose(1, 0, 2).reshape(6, width)
-    own_attn = unpack(own_attn)
-    square_total = squares[0, 0]
-    grad_norm = jnp.sqrt(square_total)
+    norms = jnp.sqrt(squares)
+    grad_norm = norms[0, 0]
     factor = jnp.minimum(1.0, clip_norm / (grad_norm + 1e-06))
-    attn_new, attn_first_new, attn_second_new = adam_step(
-        w_attn, own_attn, attn_first, attn_second, factor
-    )
-    mlp_new, mlp_first_new, mlp_second_new = adam_step(
-        w_mlp, own_mlp, mlp_first, mlp_second, factor
+    (
+        attn_new,
+        attn_copy,
+        attn_first_new,
+        attn_second_new,
+        mlp_new,
+        mlp_copy,
+        mlp_first_new,
+        mlp_second_new,
+    ) = adam(
+        norms,
+        own_attn,
+        own_up,
+        own_down,
+        (w_attn, attn_first, attn_second),
+        (w_mlp, mlp_first, mlp_second),
     )
     table_new, table_first_new, table_second_new = adam_step(
         bias_table, own_table, table_first, table_second, factor
@@ -1893,11 +1939,11 @@
         grad_words[None],
         grad_norm,
         attn_new,
-        attn_new.astype(bf16),
+        attn_copy,
         attn_first_new,
         attn_second_new,
         mlp_new,
-        mlp_new.astype(bf16),
+        mlp_copy,
         mlp_first_new,
         mlp_second_new,
         table_new,

time: 637 us -> 615 us (0.965)
  Pallas kernels: 597 us -> 577 us
  other arithmetic: 12.5 us -> 5.73 us
    pallas_call x4, Pallas kernels: 553 us -> 527 us  [move(): pl.pallas_call(functools.partial(kernel, grid), name=name, out_shape=out_...]
    convert_element_type x2 -> x0, other arithmetic: 6.63 us -> none  [the longest x1 3.68 us: body(): attn_new.astype(bf16)]
    pallas_call x0 -> x1, Pallas kernels: none -> 6.5 us  [adam(): pl.pallas_call(adam_kernel, name='adam', grid=(2, rows // part), out_shap...]
where the time goes in v2:
time: 615 us; the launch traced here: 606 us
  Pallas kernels  577 us (94%)
  local copies, waits for them, and re-layouts  21.9 us (4%)
    pallas_call x4, Pallas kernels, move(): pl.pallas_call(functools.partial(kernel, grid), name=name, out_shape=out_...  527 us
    pallas_call x1, Pallas kernels, mlp(): pl.pallas_call(mlp_kernel, name='mlp', grid=(np_,), out_shape=[jax.ShapeD...  43.5 us

profile of v2, /device:TPU:0, one launch (start us, length us, event | category | flops | bytes accessed | tf_op | source)
XLA Modules:
  0.0 606.4 jit_solution(8195333359890438605)
XLA Ops:
  0.7 1.5 convert_element_type.17.refs_4_
  2.1 1.4 convert_element_type.16
  3.5 0.9 slice_bitcast_fusion
  5.2 1.0 squeeze.34.refs_1_
  6.2 1.0 squeeze.33.refs_0_
  7.3 226.7 %attention.1 = (bf16[2,2,4,2,144,1152]{5,4,3,2,1,0:T(8,128)(2,1)}, bf16[2,2,4,2,144,1152]{5,4,3,2,1,0:T(8,128)(2,1)}, bf16[2,2,4,2,144,1152]{5,4,3,2,1,0:T(8,128...) custom-call(bf16[144,1152]{1,0:T(8,128)(2,1)} %squeeze.33.refs_0_, ...), custom_call_target="tpu_custom_call" | custom-call | flops 5435817984 | bytes 62914560 | tf_op jit(solution)/shard_map/attention/pallas_call | solution.py:765
  234.7 0.9 slice.48
  238.3 43.5 %mlp.1 = (bf16[384,1152]{1,0:T(8,128)(2,1)}, f32[384,1152]{1,0:T(8,128)}, bf16[4,1152,1152]{2,1,0:T(8,128)(2,1)}, bf16[4,1152,1152]{2,1,0:T(8,128)(2,1)}, f32[4,1,1152]{2,1,0:T(1,128)}, /*index=5*/f32[8,1152]{1,0:T(8,128)}) custom-call(bf16[384,1152]{1,0:T(8,128)(2,1)} %get-tuple-element.67.a2, bf16[384,1152]{1,0:T(8,128)(2,1)} %bitcast.39, ...), custom_call_target="tpu_custom_call" | custom-call | flops 24461180928 | bytes 46137344 | tf_op jit(solution)/shard_map/mlp/pallas_call | solution.py:1286
  281.8 69.7 %cross_backward.1 = (f32[384,1152]{1,0:T(8,128)}, bf16[1152,384]{1,0:T(8,128)(2,1)}, bf16[4,384,288]{2,1,0:T(8,128)(2,1)}, bf16[128,2304]{1,0:T(8,128)(2,1)}, f3...) custom-call(f32[384,1152]{1,0:T(8,128)} %get-tuple-element.75.refs_0_, ...), custom_call_target="tpu_custom_call" | custom-call | flops 5605687296 | bytes 52428800 | tf_op jit(solution)/shard_map/cross_backward/pallas_call | solution.py:765
  351.5 138.1 %attention_back.1 = (f32[1,144,1152]{2,1,0:T(8,128)}, bf16[4,144,1152]{2,1,0:T(8,128)(2,1)}, bf16[8,2,3,72,384]{4,3,2,1,0:T(8,128)(2,1)}, bf16[8,16,2304]{2,1,0:T(8,128)(2,1)}) custom-call(bf16[2,2,4,2,144,1152]{5,4,3,2,1,0:T(8,128)(2,1)} %bitcast.55, bf16[2,2,4,2,144,1152]{5,4,3,2,1,0:T(8,128)(2,1)} %bitcast.50, bf16[8,2,72,384]{3,2,1,0:T(8,128)(2,1)} %bitcast.51, ...), custom_call_target="tpu_custom_call" | custom-call | flops 13589544960 | bytes 62914560 | tf_op jit(solution)/shard_map/attention_back/pallas_call | solution.py:765
  489.7 92.3 %last_sums.1 = (f32[2,144,1152]{2,1,0:T(8,128)}, f32[384,1152]{1,0:T(8,128)}, f32[120,1152]{1,0:T(8,128)}, f32[8,17,144]{2,1,0:T(8,128)}, f32[17,144]{1,0:T(8,128)}, /*index=5*/f32[8,128]{1,0:T(8,128)}) custom-call(bf16[384,1152]{1,0:T(8,128)(2,1)} %get-tuple-element.73.a1, bf16[8,2,3,72,384]{4,3,2,1,0:T(8,128)(2,1)} %get-tuple-element.91.grad_qkv, ...), custom_call_target="tpu_custom_call" | custom-call | tf_op jit(solution)/shard_map/last_sums/pallas_call | solution.py:765
  582.0 1.3 slice.57
  585.2 1.4 fusion.1
  586.6 0.8 slice_bitcast_fusion.2
  588.2 1.1 copy-done.3
  589.3 1.1 copy-done.4
  590.4 1.5 copy-done.5
  591.8 1.5 copy-done.6
  593.3 1.3 copy-done.7
  594.6 1.3 copy-done.8
  596.0 1.3 copy-done.9
  597.3 6.5 %adam.1 = (f32[8,144,288]{2,1,0:T(8,128)}, bf16[8,144,288]{2,1,0:T(8,128)(2,1)}, f32[8,144,288]{2,1,0:T(8,128)}, f32[8,144,288]{2,1,0:T(8,128)}, f32[2,144,1152]...) custom-call(f32[8,128]{1,0:T(8,128)S(1)} %sqrt.6.norm, ...), custom_call_target="tpu_custom_call" | custom-call | flops 13271040 | bytes 25165824 | tf_op jit(solution)/shard_map/adam/pallas_call | solution.py:1771
  603.8 1.2 copy.39
  605.2 0.8 copy.40
  (37 shorter events, 6.3 us)
Async XLA Ops:
  0.7 3.8 copy-start
  7.3 228.4 %copy-start.15 = (bf16[1,6,1152]{2,1,0:T(8,128)(2,1)S(1)}, bf16[1,6,1152]{2,1,0:T(8,128)(2,1)}, u32[]{:S(2)}) copy-start(bf16[1,6,1152]{2,1,0:T(8,128)(2,1)} %param.14) | copy-start | bytes 41476
  489.7 95.5 %copy-start.12 = (f32[17,144]{1,0:T(8,128)S(1)}, f32[17,144]{1,0:T(8,128)}, u32[]{:S(2)}) copy-start(f32[17,144]{1,0:T(8,128)} %param.19) | copy-start | bytes 29380
  489.7 95.5 %copy-start.13 = (f32[17,144]{1,0:T(8,128)S(1)}, f32[17,144]{1,0:T(8,128)}, u32[]{:S(2)}) copy-start(f32[17,144]{1,0:T(8,128)} %param.24) | copy-start | bytes 29380
  489.7 95.5 %copy-start.14 = (f32[17,144]{1,0:T(8,128)S(1)}, f32[17,144]{1,0:T(8,128)}, u32[]{:S(2)}) copy-start(f32[17,144]{1,0:T(8,128)} %param.25) | copy-start | bytes 29380
  489.7 98.5 %copy-start.1 = (f32[8,144,288]{2,1,0:T(8,128)S(1)}, f32[8,144,288]{2,1,0:T(8,128)}, u32[]{:S(2)}) copy-start(f32[8,144,288]{2,1,0:T(8,128)} %w_attn.1) | copy-start | bytes 3981316
  489.7 98.5 %copy-start.2 = (f32[2,144,1152]{2,1,0:T(8,128)S(1)}, f32[2,144,1152]{2,1,0:T(8,128)}, u32[]{:S(2)}) copy-start(f32[2,144,1152]{2,1,0:T(8,128)} %w_mlp.1) | copy-start | bytes 3981316
  588.2 1.1 copy-start.3
  589.3 1.1 copy-start.4
  590.4 1.5 copy-start.5
  591.8 1.5 copy-start.6
  593.3 1.3 copy-start.7
  594.6 1.3 copy-start.8
  596.0 1.3 copy-start.9
  597.3 6.5 %copy-start.10 = (f32[384,1152]{1,0:T(8,128)S(1)}, f32[384,1152]{1,0:T(8,128)}, u32[]{:S(2)}) copy-start(f32[384,1152]{1,0:T(8,128)} %get-tuple-element.102) | copy-start | bytes 5308420
  603.8 1.4 copy-start.11
